TPU v7x, 512 devices: a whole 4x4x16 slice. The times are simulated.
512 devices in a mesh: lat: 16 (over x_lo, y, core), lon: 32 (over z, x_hi).
Axes of the slice: x: 4 (x_hi: 2, x_lo: 2; x = x_hi * 2 + x_lo), y: 4, z: 16, core: 2. Of those that a mesh axis runs over, the one named last changes fastest.
Arguments:
- tokens: bfloat16 [4, 192, 768, 512], P(None, 'lat', 'lon'), may hold values from -20 to 20
- region: int32 [4, 192, 768], P(None, 'lat', 'lon'), may hold values from 0 to 7
- qkv_weight: bfloat16 [512, 1536], P('lat', 'lon'), may hold values from -1 to 1
- proj_weight: bfloat16 [512, 512], P('lat', 'lon'), may hold values from -1 to 1
Outputs:
- blended: bfloat16 [4, 192, 768, 512], P(None, 'lat', 'lon')
All inputs are finite; a program needn't handle non-finite values.
Results may differ from a plain program's by a relative error of at most 0.0066.
Values may be sent and summed in bfloat16 or wider, within the bound.
A program may use at most 64 MiB of HBM per device.

v0:
```python
import jax
import jax.numpy as jnp
from jax import lax
from jax.sharding import PartitionSpec as P

HEADS = 8
WLEV = 2
WLAT = 6
WLON = 12


epsilon = 1e-05


def passed_along(block, axis, distance):
    devices = range(lax.axis_size(axis))
    route = [((i - distance) % len(devices), i) for i in devices]
    return lax.ppermute(block, axis, route)


def layer_normed(grid):
    floated = grid.astype(jnp.float32)
    average = jnp.mean(floated, axis=-1, keepdims=True)
    centred = floated - average
    spread = jnp.mean(centred * centred, axis=-1, keepdims=True)
    return (centred * lax.rsqrt(spread + epsilon)).astype(jnp.bfloat16)


def to_windows(grid):
    level_n, lat_n, lon_n, channels = grid.shape
    shaped = grid.reshape(level_n // WLEV, WLEV, lat_n // WLAT, WLAT, lon_n // WLON, WLON, channels)
    return shaped.transpose(0, 2, 4, 1, 3, 5, 6).reshape(-1, WLEV * WLAT * WLON, channels)


def from_windows(groups, level_n, lat_n, lon_n):
    channels = groups.shape[-1]
    shaped = groups.reshape(
        level_n // WLEV, lat_n // WLAT, lon_n // WLON, WLEV, WLAT, WLON, channels
    )
    return shaped.transpose(0, 3, 1, 4, 2, 5, 6).reshape(level_n, lat_n, lon_n, channels)


def windowed(qkv_grid, labels):
    level_n, lat_n, lon_n, triple = qkv_grid.shape
    features = triple // 3
    grouped = to_windows(qkv_grid)
    tags = to_windows(labels[..., None])[..., 0]
    allowed = tags[:, :, None] == tags[:, None, :]
    window_n, span_n = (grouped.shape[0], grouped.shape[1])
    split_heads = grouped.reshape(window_n, span_n, 3, HEADS, features // HEADS).transpose(
        2, 3, 0, 1, 4
    )
    factor = (features // HEADS) ** (-0.5)

    def one_head(triplet):
        queries, key_rows, value_rows = triplet
        scores = (
            jnp.einsum("wqd,wkd->wqk", queries, key_rows, preferred_element_type=jnp.float32)
            * factor
        )
        scores = jnp.where(allowed, scores, -jnp.inf)
        highest = jnp.max(scores, axis=-1, keepdims=True)
        raised = jnp.exp(scores - highest)
        chances = (raised / jnp.sum(raised, axis=-1, keepdims=True)).astype(jnp.bfloat16)
        mixed_rows = jnp.einsum(
            "wqk,wkd->wqd", chances, value_rows, preferred_element_type=jnp.float32
        )
        return mixed_rows.astype(jnp.bfloat16)

    per_head = lax.map(one_head, (split_heads[0], split_heads[1], split_heads[2]))
    joined = per_head.transpose(1, 2, 0, 3).reshape(window_n, span_n, features)
    return from_windows(joined, level_n, lat_n, lon_n)


def local(tokens, region, qkv_weight, proj_weight):
    level_n, lat_rows, lon_cols, features = tokens.shape
    half_lat = WLAT // 2
    half_lon = WLON // 2
    turned = jnp.roll(tokens, -(WLEV // 2), axis=0)
    eastern = passed_along(turned[:, :, :half_lon], "lon", -1)
    widened = jnp.concatenate((turned[:, :, half_lon:], eastern), axis=2)
    southern = passed_along(widened[:, :half_lat], "lat", -1)
    shifted = jnp.concatenate((widened[:, half_lat:], southern), axis=1)
    normed = layer_normed(shifted).reshape(-1, features)
    column_qkv, column_proj = (
        lax.all_gather(qkv_weight, "lon", axis=1, tiled=True),
        lax.all_gather(proj_weight, "lon", axis=1, tiled=True),
    )
    whole_qkv, whole_proj = (
        lax.all_gather(column_qkv, "lat", axis=0, tiled=True),
        lax.all_gather(column_proj, "lat", axis=0, tiled=True),
    )
    qkv = jnp.dot(normed, whole_qkv, preferred_element_type=jnp.float32).astype(jnp.bfloat16)
    attended = windowed(qkv.reshape(level_n, lat_rows, lon_cols, 3 * features), region)
    backward = jnp.roll(attended, WLEV // 2, axis=0)
    northern = passed_along(backward[:, lat_rows - half_lat :], "lat", 1)
    lowered = jnp.concatenate((northern, backward[:, : lat_rows - half_lat]), axis=1)
    western = passed_along(lowered[:, :, lon_cols - half_lon :], "lon", 1)
    restored = jnp.concatenate((western, lowered[:, :, : lon_cols - half_lon]), axis=2).reshape(
        -1, features
    )
    branch = jnp.dot(restored, whole_proj, preferred_element_type=jnp.float32)
    summed = tokens.reshape(-1, features).astype(jnp.float32) + branch
    return summed.astype(jnp.bfloat16).reshape(tokens.shape)


def solution(mesh):
    placed = (P(None, "lat", "lon", None), P(None, "lat", "lon"), P("lat", "lon"), P("lat", "lon"))
    return jax.shard_map(
        local, mesh=mesh, in_specs=placed, out_specs=P(None, "lat", "lon", None), check_vma=False
    )
```

profile of v0, /device:TPU:6, one launch (start us, length us, event | category | flops | bytes accessed | tf_op | source)
XLA Modules:
  0.0 321.5 jit_solution(17681184874477554477)
XLA Ops:
  6.5 80.4 %all-gather = bf16[32,48,32]{1,2,0:T(8,128)(2,1)S(1)} all-gather(bf16[1,48,32]{1,2,0:T(8,128)(2,1)} %bitcast.90), channel_id=1, replica_groups=mesh['lat'=16,'lon'=32] {'lon'}, dimensions={0}, use_global_device_ids=true | all-gather | bytes 101376 | tf_op jit(solution)/shard_map/all_gather | solution.py:86
  88.2 6.3 %collective-permute-start = (bf16[4,12,6,512]{3,2,1,0:T(8,128)(2,1)S(1)}, bf16[4,12,6,512]{3,2,1,0:T(8,128)(2,1)S(1)}, u32[]{:S(2)}, u32[]{:S(2)}) collective-permute-start(bf16[4,12,6,512]{3,2,1,0:T(8,128)(2,1)S(1)} %pad_maximum_fusion.2), channel_id=1, source_target_pairs={{1,0},{2,1},{3,2},{4,3},{5,4},{6,5},{7,6},{8,7},{9,8},{10,9},{11,1... | collective-permute-start | bytes 884744 | tf_op jit(solution)/shard_map/ppermute | solution.py:18
  94.9 5.4 %collective-permute-done = bf16[4,12,6,512]{3,2,1,0:T(8,128)(2,1)S(1)} collective-permute-done((bf16[4,12,6,512]{3,2,1,0:T(8,128)(2,1)S(1)}, bf16[4,12,6,512]{3,2,1,0:T(8,128)(2,1)S(1)}, u32[]{:S(2)}, u32[]{:S(2)}) %collective-permute-start) | collective-permute-done | bytes 294944 | tf_op jit(solution)/shard_map/ppermute | solution.py:18
  100.4 1.9 collective-permute-start.1
  102.7 5.0 %collective-permute-done.1 = bf16[4,3,24,512]{3,2,1,0:T(8,128)(2,1)S(1)} collective-permute-done((bf16[4,3,24,512]{3,2,1,0:T(8,128)(2,1)S(1)}, bf16[4,3,24,512]{3,2,1,0:T(8,128)(2,1)S(1)}, u32[]{:S(2)}, u32[]{:S(2)}) %collective-permute-start.1) | collective-permute-done | bytes 294944 | tf_op jit(solution)/shard_map/ppermute | solution.py:18
  110.2 16.4 %all-gather.3.cloned.1.call-done = bf16[512,1536]{1,0:T(8,128)(2,1)} async-done(((bf16[32,1536]{1,0:T(8,128)(2,1)}), bf16[512,1536]{1,0:T(8,128)(2,1)}) %all-gather.3.cloned.1.call-update) | async-done | bytes 1572880 | tf_op jit(solution)/shard_map/all_gather | solution.py:90
  126.6 3.8 %convolution_convert_fusion.1 = bf16[1152,1536]{1,0:T(8,128)(2,1)S(1)} fusion(bf16[1152,512]{1,0:T(8,128)(2,1)} %fusion.31, bf16[512,1536]{1,0:T(8,128)(2,1)} %all-gather.3.cloned.1.call-done), kind=kOutput, calls=%fused_computation.22 | convolution fusion | flops 1813708800 | bytes 6291456 | tf_op jit(solution)/shard_map/dot_general | solution.py:93
  130.4 3.6 %reshape_reshape.9 = bf16[2,2,2,6,2,12,1536]{6,5,4,3,2,1,0:T(8,128)(2,1)} reshape(bf16[1152,1536]{1,0:T(8,128)(2,1)S(1)} %convolution_convert_fusion.1) | data formatting | bytes 7077888 | tf_op jit(solution)/shard_map/reshape;reshape | solution.py:31
  133.9 6.0 %copy.39 = bf16[2,2,2,2,6,12,1536]{6,2,1,0,5,4,3:T(2,128)(2,1)S(1)} copy(bf16[2,2,2,2,6,12,1536]{6,5,2,4,1,3,0:T(8,128)(2,1)} %bitcast.83) | data formatting | bytes 7077888 | tf_op jit(solution)/shard_map/transpose | solution.py:32
  139.9 6.9 %reshape_reshape.10 = bf16[8,144,3,8,64]{4,3,2,0,1:T(8,128)(2,1)} reshape(bf16[2,2,2,2,6,12,1536]{6,2,1,0,5,4,3:T(2,128)(2,1)S(1)} %copy.39) | data formatting | bytes 7077888 | tf_op jit(solution)/shard_map/reshape;reshape | solution.py:50
  146.8 7.8 %slice_bitcast_fusion = (bf16[8,8,144,64]{3,0,1,2:T(8,128)(2,1)S(1)}, bf16[8,8,144,64]{3,0,1,2:T(8,128)(2,1)}, bf16[8,8,144,64]{3,0,1,2:T(8,128)(2,1)}) fusion(bf16[3,8,8,144,64]{4,1,0,2,3:T(8,128)(2,1)} %bitcast.79), kind=kLoop, calls=%fused_computation.25 | loop fusion | bytes 7077888 | tf_op jit(solution)/shard_map/squeeze | solution.py:70
  154.7 4.8 %copy.41 = bf16[8,8,144,64]{2,3,1,0:T(8,128)(2,1)} copy(bf16[8,8,144,64]{3,0,1,2:T(8,128)(2,1)} %get-tuple-element.93) | data formatting | bytes 2359296
  159.4 4.8 %copy.42 = bf16[8,8,144,64]{2,3,1,0:T(8,128)(2,1)} copy(bf16[8,8,144,64]{3,0,1,2:T(8,128)(2,1)} %get-tuple-element.92) | data formatting | bytes 2359296
  164.3 3.3 %copy.43 = bf16[8,8,144,64]{2,3,1,0:T(8,128)(2,1)} copy(bf16[8,8,144,64]{3,0,1,2:T(8,128)(2,1)S(1)} %get-tuple-element.91) | data formatting | bytes 2359296
  167.6 28.3 %while.11 = (s32[]{:T(128)}, bf16[8,8,144,64]{2,3,1,0:T(8,128)(2,1)}, bf16[8,8,144,64]{2,3,1,0:T(8,128)(2,1)}, bf16[8,8,144,64]{2,3,1,0:T(8,128)(2,1)}, bf16[8,8...) while((s32[]{:T(128)}, bf16[8,8,144,64]{2,3,1,0:T(8,128)(2,1)}, ...), condition=%wide.region_5.6_spmd.clone, body=%wide.region_2.5_spmd.clone.sunk | while | flops 43702416 | bytes 2403405 | solution.py:70
  179.8 1.9 fusion.53
  183.4 1.9 fusion.53
  186.9 1.9 fusion.53
  195.9 3.8 %copy.44 = bf16[8,144,8,64]{3,2,0,1:T(8,128)(2,1)S(1)} copy(bf16[8,144,8,64]{1,3,0,2:T(8,128)(2,1)} %bitcast.85) | data formatting | bytes 2359296 | tf_op jit(solution)/shard_map/transpose | solution.py:71
  203.7 2.4 collective-permute-start.2
  206.1 7.8 %collective-permute-done.2 = bf16[4,3,24,512]{3,0,2,1:T(4,128)(2,1)S(1)} collective-permute-done((bf16[4,3,24,512]{3,0,2,1:T(4,128)(2,1)S(1)}, bf16[4,3,24,512]{3,0,2,1:T(4,128)(2,1)S(1)}, u32[]{:S(2)}, u32[]{:S(2)}) %collective-permute-start.2) | collective-permute-done | bytes 294944 | tf_op jit(solution)/shard_map/ppermute | solution.py:18
  214.1 4.2 %collective-permute-start.3 = (bf16[4,12,6,512]{3,0,2,1:T(4,128)(2,1)S(1)}, bf16[4,12,6,512]{3,0,2,1:T(4,128)(2,1)S(1)}, u32[]{:S(2)}, u32[]{:S(2)}) collective-permute-start(bf16[4,12,6,512]{3,0,2,1:T(4,128)(2,1)S(1)} %pad_maximum_fusion.3), channel_id=1, source_target_pairs={{31,0},{0,1},{1,2},{2,3},{3,4},{4,5},{5,6},{6,7},{7,8},{8,9},{9,10... | collective-permute-start | bytes 884744 | tf_op jit(solution)/shard_map/ppermute | solution.py:18
  218.4 73.6 %all_gather.14 = bf16[32,512]{0,1:T(8,128)(2,1)S(1)} all-gather(bf16[32,16]{0,1:T(8,128)(2,1)S(1)} %copy-done.3), channel_id=1, replica_groups=mesh['lat'=16,'lon'=32] {'lon'}, dimensions={1}, use_global_device_ids=true | all-gather | bytes 33792 | tf_op jit(solution)/shard_map/all_gather | solution.py:87
  292.1 18.6 %all_gather.15 = bf16[512,512]{1,0:T(8,128)(2,1)S(1)} all-gather(bf16[32,512]{1,0:T(8,128)(2,1)S(1)} %copy.47), channel_id=1, replica_groups=mesh['lat'=16,'lon'=32] {'lat'}, dimensions={0}, use_global_device_ids=true | all-gather | bytes 557056 | tf_op jit(solution)/shard_map/all_gather | solution.py:91
  (54 shorter events, 35.3 us)
Async XLA Ops:
  6.5 81.5 %copy-start = (bf16[4,12,24,512]{3,2,1,0:T(8,128)(2,1)S(1)}, bf16[4,12,24,512]{3,2,1,0:T(8,128)(2,1)}, u32[]{:S(2)}) copy-start(bf16[4,12,24,512]{3,2,1,0:T(8,128)(2,1)} %param.6) | copy-start | bytes 3538948
  6.5 120.1 %all-gather.3.cloned.1.call-start = ((), (), s32[]{:S(2)}) async-start(), calls=%async_computation | async-start | bytes 1671168 | tf_op jit(solution)/shard_map/all_gather | solution.py:90
  88.2 14.1 %copy-start.2 = (s32[4,12,24]{2,0,1:T(4,128)S(1)}, s32[4,12,24]{2,0,1:T(4,128)}, u32[]{:S(2)}) copy-start(s32[4,12,24]{2,0,1:T(4,128)} %param.7) | copy-start | bytes 13828
  88.2 12.1 %collective-permute-start = (bf16[4,12,6,512]{3,2,1,0:T(8,128)(2,1)S(1)}, bf16[4,12,6,512]{3,2,1,0:T(8,128)(2,1)S(1)}, u32[]{:S(2)}, u32[]{:S(2)}) collective-permute-start(bf16[4,12,6,512]{3,2,1,0:T(8,128)(2,1)S(1)} %pad_maximum_fusion.2), channel_id=1, source_target_pairs={{1,0},{2,1},{3,2},{4,3},{5,4},{6,5},{7,6},{8,7},{9,8},{10,9},{11,1... | collective-permute-start | bytes 884744 | tf_op jit(solution)/shard_map/ppermute | solution.py:18
  100.4 7.4 %collective-permute-start.1 = (bf16[4,3,24,512]{3,2,1,0:T(8,128)(2,1)S(1)}, bf16[4,3,24,512]{3,2,1,0:T(8,128)(2,1)S(1)}, u32[]{:S(2)}, u32[]{:S(2)}) collective-permute-start(bf16[4,3,24,512]{3,2,1,0:T(8,128)(2,1)S(1)} %pad_maximum_fusion.5), channel_id=1, source_target_pairs={{32,0},{64,32},{96,64},{128,96},{160,128},{192,160},{224,192},{256... | collective-permute-start | bytes 884744 | tf_op jit(solution)/shard_map/ppermute | solution.py:18
  203.7 14.7 %copy-start.3 = (bf16[32,16]{0,1:T(8,128)(2,1)S(1)}, bf16[32,16]{0,1:T(8,128)(2,1)}, u32[]{:S(2)}) copy-start(bf16[32,16]{0,1:T(8,128)(2,1)} %param.9) | copy-start | bytes 3076
  203.7 10.2 %collective-permute-start.2 = (bf16[4,3,24,512]{3,0,2,1:T(4,128)(2,1)S(1)}, bf16[4,3,24,512]{3,0,2,1:T(4,128)(2,1)S(1)}, u32[]{:S(2)}, u32[]{:S(2)}) collective-permute-start(bf16[4,3,24,512]{3,0,2,1:T(4,128)(2,1)S(1)} %pad_maximum_fusion.4), channel_id=1, source_target_pairs={{480,0},{0,32},{32,64},{64,96},{96,128},{128,160},{160,192},{192,2... | collective-permute-start | bytes 884744 | tf_op jit(solution)/shard_map/ppermute | solution.py:18
  214.1 96.5 %collective-permute-start.3 = (bf16[4,12,6,512]{3,0,2,1:T(4,128)(2,1)S(1)}, bf16[4,12,6,512]{3,0,2,1:T(4,128)(2,1)S(1)}, u32[]{:S(2)}, u32[]{:S(2)}) collective-permute-start(bf16[4,12,6,512]{3,0,2,1:T(4,128)(2,1)S(1)} %pad_maximum_fusion.3), channel_id=1, source_target_pairs={{31,0},{0,1},{1,2},{2,3},{3,4},{4,5},{5,6},{6,7},{7,8},{8,9},{9,10... | collective-permute-start | bytes 884744 | tf_op jit(solution)/shard_map/ppermute | solution.py:18
  311.6 1.3 copy-start.1
Sparse Core Ops, SparseCore 0:
  88.2 38.3 all-gather.2
where the time goes:
time: 326 us; the launch traced here: 322 us
  blocking collectives  173 us (53%)
  local copies, waits for them, and re-layouts  47.5 us (15%)
  waiting for transfers between devices  34.6 us (11%)
  matrix products  33.8 us (10%)
  starting transfers between devices  14.9 us (5%)
  between operations  13.7 us (4%)
  other arithmetic  4.41 us (1%)
    all_gather x1, blocking collectives, local(): lax.all_gather(qkv_weight, 'lon', axis=1, tiled=True)  80.4 us
    all_gather x1, blocking collectives, local(): lax.all_gather(proj_weight, 'lon', axis=1, tiled=True)  73.6 us
    all_gather x1, blocking collectives, local(): lax.all_gather(column_proj, 'lat', axis=0, tiled=True)  18.6 us
    ppermute x4, waiting for transfers between devices, passed_along(): return lax.ppermute(block, axis, route)  18.2 us
    all_gather x1, waiting for transfers between devices, local(): lax.all_gather(column_qkv, 'lat', axis=0, tiled=True)  16.4 us
    dot_general x8, matrix products, one_head(): jnp.einsum('wqk,wkd->wqd', chances, value_rows, preferred_element_type=jn...  15.2 us
    unnamed x12, local copies, waits for them, and re-layouts  15 us
    ppermute x4, starting transfers between devices, passed_along(): return lax.ppermute(block, axis, route)  14.9 us
  transfers between devices with their start and end apart: 5, of which 4 were waited for; matrix products, arithmetic and copies ran while one was open for 1% of the time, Pallas kernels for 0%

commit v1 on v0

v1 whole, which is shorter than its diff:
```python
import jax
import jax.numpy as jnp
import numpy as np
from jax import lax
from jax.experimental import pallas as pl
from jax.experimental.pallas import tpu as pltpu
from jax.sharding import PartitionSpec as P

MESH = pl.DeviceIdType.MESH
BF16 = jnp.bfloat16
F32 = jnp.float32

LEVELS, ROWS, COLS, D = 4, 12, 24, 512
HEADS = 8
LEVEL = ROWS * COLS
SPAN = 144
EPS = 1e-05
SCALE = float(np.log2(np.e) / 8.0)

RELATIVE = [0, 1, 2, 3, 4, -1, -2, -3, -4, 5, 6, 7, 8, -5, -6, -7]
PARTS = ((0, 9), (9, 7))


def positions(levels, rows, cols, pad=0):
    found = [(l, a, o) for l in levels for a in rows for o in cols]
    return found + [None] * pad


def one_hot(dest, source):
    where = {place: i for i, place in enumerate(source) if place is not None}
    matrix = np.zeros((len(dest), len(source)), np.float32)
    for i, place in enumerate(dest):
        if place in where:
            matrix[i, where[place]] = 1.0
    return matrix


BOTH = (0, 1)
OWN = positions(BOTH, range(ROWS), range(COLS))
W_PACK = positions(BOTH, range(3, 12), range(6), 4)
N_PACK = positions(BOTH, range(3), range(6, 24), 4)
C_PACK = positions(BOTH, range(3), range(6), 12)
E_SIDE = positions(BOTH, range(3, 12), range(24, 30), 4)
S_SIDE = positions(BOTH, range(12, 15), range(6, 24), 4)
C_SIDE = positions(BOTH, range(12, 15), range(24, 30), 12)
WINDOWS = [
    positions(BOTH, range(3 + 6 * i, 9 + 6 * i), range(6 + 12 * j, 18 + 12 * j))
    for i in (1, 0)
    for j in (1, 0)
]

PACKS = [one_hot(pack, OWN) for pack in (W_PACK, N_PACK, C_PACK)]
GATHERS = [one_hot(window, OWN) for window in WINDOWS]
SIDES = [
    [one_hot(WINDOWS[0], E_SIDE), one_hot(WINDOWS[0], S_SIDE), one_hot(WINDOWS[0], C_SIDE)],
    [None, one_hot(WINDOWS[1], S_SIDE), None],
    [one_hot(WINDOWS[2], E_SIDE), None, None],
    [None, None, None],
]


def lane_moves():
    moves = np.zeros((4, 128, 512), np.float32)
    for m in range(4):
        for q in range(4):
            for k in range(32):
                moves[m, q * 32 + k, q * 128 + m * 32 + k] = 1.0
    return moves


SLABS = {0: (208, 80), 1: (208, 80), 2: (64, 160), 3: (64, 160)}


def own_level(pair, part):
    return (2 * pair + part + 1) % LEVELS


def nn(a, b):
    return lax.dot_general(a, b, (((1,), (0,)), ((), ())), preferred_element_type=F32)


def nt(a, b):
    return lax.dot_general(a, b, (((1,), (1,)), ((), ())), preferred_element_type=F32)


def kernel(
    tokens, tile, tag_rows, tag_cols, packs, gathers, sides, moves, packs_t, gathers_t, sides_t,
    out,
    normed, windows, qkv, attended, restored, raw, whole_qkv, whole_proj,
    w_out, n_out, c_out, w_in, n_in, c_in, w_back, n_back, c_back, w_home, n_home, c_home,
    z_send, z_recv, p_send, p_recv, core_send, core_recv, halo_send, halo_recv, back_send, back_recv,
):
    lat = lax.axis_index("lat")
    lon = lax.axis_index("lon")
    core = lat % 2
    y = (lat // 2) % 4
    x = (lon % 2) * 2 + lat // 8
    z = lon // 2

    def at(xx, yy, zz, cc):
        return ((xx % 2) * 8 + yy * 2 + cc, zz * 2 + xx // 2)

    def along_z(step):
        return at(x, y, (z + step + 16) % 16, core)

    def in_plane(j):
        return at((x + j // 4) % 4, (y + j % 4) % 4, z, core)

    def beside(d_lat, d_lon):
        return ((lat + d_lat + 16) % 16, (lon + d_lon + 32) % 32)

    peer = at(x, y, z, 1 - core)
    near = [s for s in RELATIVE if 0 < abs(s) <= 4]
    partners = [along_z(s) for s in near]
    partners += [peer]
    partners += [beside(a, b) for a, b in ((0, 1), (0, -1), (1, 0), (-1, 0), (1, 1), (-1, -1))]
    barrier = pltpu.get_barrier_semaphore()
    for partner in partners:
        pl.semaphore_signal(barrier, 1, device_id=partner, device_id_type=MESH)

    @pl.loop(1, 16)
    def _(j):
        pl.semaphore_signal(barrier, 1, device_id=in_plane(j), device_id_type=MESH)

    raw[0, 0, 0] = tile[...]

    @pl.loop(0, 24)
    def _(i):
        rows = pl.ds(pl.multiple_of(i * 48, 48), 48)
        floated = tokens[rows, :].astype(F32)
        average = jnp.mean(floated, axis=-1, keepdims=True)
        centred = floated - average
        spread = jnp.mean(centred * centred, axis=-1, keepdims=True)
        normed[rows, :] = (centred * lax.rsqrt(spread + EPS)).astype(BF16)

    def slab(pair, part, start, size):
        return normed[pl.ds(own_level(pair, part) * LEVEL + start, size), :]

    for pair in range(2):
        for buf, first, size, start, height in (
            (w_out, 0, 112, 64, 224), (n_out, 112, 112, 0, 80), (c_out, 224, 48, 0, 80),
        ):
            total = 0.0
            for part in range(2):
                chosen = packs[pl.ds(first, size), pl.ds(part * LEVEL, LEVEL)][:, start:start + height]
                total += nn(chosen, slab(pair, part, start, height))
            buf[pl.ds(pair * size, size), :] = total.astype(BF16)

    pl.semaphore_wait(barrier, len(partners) + 15)

    def remote(src, dst, send, recv, target):
        return pltpu.make_async_remote_copy(src, dst, send, recv, device_id=target, device_id_type=MESH)

    first = []
    for n, s in enumerate(near):
        slot = RELATIVE.index(-s)
        copy = remote(raw.at[0, 0, 0], raw.at[0, 0, slot], z_send.at[n], z_recv.at[slot], along_z(s))
        copy.start()
        first.append(copy)
    halos = []
    for n, (src, dst, target) in enumerate((
        (w_out, w_in, beside(0, -1)), (c_out, c_in, beside(-1, -1)), (n_out, n_in, beside(-1, 0)),
    )):
        copy = remote(src, dst, halo_send.at[n], halo_recv.at[n], target)
        copy.start()
        halos.append(copy)
    for copy in first:
        copy.wait_recv()

    far = [
        remote(raw.at[0, 0, pl.ds(1, 4)], raw.at[0, 0, pl.ds(9, 4)], z_send.at[8], z_recv.at[9], along_z(-4)),
        remote(raw.at[0, 0, pl.ds(5, 3)], raw.at[0, 0, pl.ds(13, 3)], z_send.at[9], z_recv.at[10], along_z(4)),
    ]
    for copy in far:
        copy.start()

    def spread(part, j):
        span = pl.ds(*PARTS[part])
        back = ((4 - j // 4) % 4) * 4 + (4 - j % 4) % 4
        return remote(
            raw.at[0, 0, span], raw.at[0, back, span], p_send.at[part, j], p_recv.at[part, back], in_plane(j)
        )

    def arrival(part, j):
        span = pl.ds(*PARTS[part])
        return remote(
            raw.at[0, 0, span], raw.at[0, j, span], p_send.at[part, j], p_recv.at[part, j], in_plane(j)
        )

    def relay(part, j):
        span = pl.ds(*PARTS[part])
        return remote(
            raw.at[0, j, span], raw.at[1, j, span], core_send.at[part, j], core_recv.at[part, j], peer
        )

    def send_part(part):
        relay(part, 0).start()

        @pl.loop(1, 16)
        def _(j):
            spread(part, j).start()

    send_part(0)
    for copy in far:
        copy.wait_recv()
    send_part(1)
    for part in range(2):

        @pl.loop(1, 16)
        def _(j):
            arrival(part, j).wait_recv()
            relay(part, j).start()

    for copy in halos:
        copy.wait_recv()
    beginnings = (0, 112, 224)
    sizes = (112, 112, 48)
    for pair in range(2):
        for w in range(4):
            start, height = SLABS[w]
            total = 0.0
            for part in range(2):
                chosen = gathers[w, :, pl.ds(part * LEVEL, LEVEL)][:, start:start + height]
                total += nn(chosen, slab(pair, part, start, height))
            for k, arrived in enumerate((w_in, n_in, c_in)):
                if SIDES[w][k] is not None:
                    total += nn(
                        sides[w, :, pl.ds(k * 128, sizes[k])], arrived[pl.ds(pair * sizes[k], sizes[k]), :]
                    )
            windows[2 * w + pair] = total.astype(BF16)

    for part in range(2):

        @pl.loop(0, 16)
        def _(j):
            relay(part, j).wait_recv()

    for x_hi in range(2):
        for group in range(4):
            x_lo, y_hi = group // 2, group % 2
            total = 0.0
            for member in range(4):
                y_lo, cc = member // 2, member % 2
                j = ((x_hi * 2 + x_lo - x + 4) % 4) * 4 + (y_hi * 2 + y_lo - y + 4) % 4
                piece = raw[(cc + core) % 2, j].reshape(256, 128)
                total += nn(piece, moves[member])
            total = total.astype(BF16)
            lanes = pl.ds(group * 128, 128)
            for s in range(16):
                band = ((z + RELATIVE[s] + 16) % 16) * 2 + x_hi
                for q in range(4):
                    block = total[s * 16:(s + 1) * 16, q * 128:(q + 1) * 128]
                    if q < 3:
                        whole_qkv[pl.ds(pl.multiple_of(band * 48 + q * 16, 16), 16), lanes] = block
                    else:
                        whole_proj[pl.ds(pl.multiple_of(band * 16, 16), 16), lanes] = block

    @pl.loop(0, 6)
    def _(n):
        weights = whole_qkv[pl.ds(pl.multiple_of(n * 256, 256), 256), :]
        for w in range(8):
            qkv[n, w] = nt(windows[w], weights).astype(BF16)

    lower = lax.broadcasted_iota(jnp.int32, (SPAN, 128), 1) < 64
    ones = jnp.ones((SPAN, 128), BF16)

    def attend(w):
        bias = jnp.where(tag_cols[w] == tag_rows[w], 0.0, -1e30)
        bias = jnp.concatenate([bias, bias], axis=0)
        for t in range(4):
            lanes = slice((t % 2) * 128, (t % 2) * 128 + 128)
            query = qkv[t // 2, w, :, lanes]
            zero = jnp.zeros_like(query)
            both = jnp.concatenate([jnp.where(lower, query, zero), jnp.where(lower, zero, query)], axis=0)
            score = nt(both, qkv[2 + t // 2, w, :, lanes]) + bias
            raised = jnp.exp2((score - jnp.max(score, axis=-1, keepdims=True)) * SCALE).astype(BF16)
            mixed = nn(raised, jnp.concatenate([qkv[4 + t // 2, w, :, lanes], ones], axis=1))
            top = jnp.where(lower, mixed[:SPAN, :128], mixed[SPAN:, :128])
            bottom = jnp.where(lower, mixed[:SPAN, 128:], mixed[SPAN:, 128:])
            attended[w, :, pl.ds(t * 128, 128)] = (top / bottom).astype(BF16)

    def give_back(k, buf, sources, pair):
        total = 0.0
        for w in sources:
            total += nn(sides_t[w, pl.ds(k * 128, sizes[k]), :], attended[2 * w + pair])
        buf[pl.ds(pair * sizes[k], sizes[k]), :] = total.astype(BF16)

    returns = []

    def send_back(k, src, dst, target):
        copy = remote(src, dst, back_send.at[k], back_recv.at[k], target)
        copy.start()
        returns.append(copy)

    @pl.loop(0, 2)
    def _(w):
        attend(w)

    for pair in range(2):
        give_back(2, c_back, (0,), pair)
    send_back(2, c_back, c_home, beside(1, 1))

    @pl.loop(4, 6)
    def _(w):
        attend(w)

    for pair in range(2):
        give_back(0, w_back, (0, 2), pair)
    send_back(0, w_back, w_home, beside(0, 1))

    @pl.loop(2, 4)
    def _(w):
        attend(w)

    for pair in range(2):
        give_back(1, n_back, (0, 1), pair)
    send_back(1, n_back, n_home, beside(1, 0))

    @pl.loop(6, 8)
    def _(w):
        attend(w)

    for pair in range(2):
        for part in range(2):
            total = 0.0
            for w in range(4):
                total += nn(gathers_t[w, pl.ds(part * LEVEL, LEVEL), :], attended[2 * w + pair])
            restored[own_level(pair, part)] = total

    for copy in returns:
        copy.wait_recv()
    for pair in range(2):
        for part in range(2):
            level = own_level(pair, part)
            total = restored[level]
            for k, home in enumerate((w_home, n_home, c_home)):
                total += nn(
                    packs_t[pl.ds(part * LEVEL, LEVEL), pl.ds(k * 128, sizes[k])],
                    home[pl.ds(pair * sizes[k], sizes[k]), :],
                )
            branch = nt(total.astype(BF16), whole_proj[...])
            rows = pl.ds(level * LEVEL, LEVEL)
            out[rows, :] = (tokens[rows, :].astype(F32) + branch).astype(BF16)

    for copy in first + far + halos + returns:
        copy.wait_send()
    for part in range(2):
        relay(part, 0).wait_send()

        @pl.loop(1, 16)
        def _(j):
            spread(part, j).wait_send()
            relay(part, j).wait_send()


def constants():
    packs = np.concatenate(PACKS, axis=0)
    gathers = np.stack(GATHERS)
    sides = np.zeros((3, SPAN, 384), np.float32)
    for w in range(3):
        for k, matrix in enumerate(SIDES[w]):
            if matrix is not None:
                sides[w, :, k * 128:k * 128 + matrix.shape[1]] = matrix
    packs_t = np.zeros((2 * LEVEL, 384), np.float32)
    for k, matrix in enumerate(PACKS):
        packs_t[:, k * 128:k * 128 + matrix.shape[0]] = matrix.T
    return [
        jnp.asarray(a, BF16)
        for a in (packs, gathers, sides, lane_moves(), packs_t, gathers.transpose(0, 2, 1), sides.transpose(0, 2, 1))
    ]


def local(tokens, region, qkv_weight, proj_weight):
    tile = jnp.concatenate([qkv_weight, proj_weight], axis=1).T
    tile = tile.reshape(4, 16, 32).transpose(1, 0, 2).reshape(16, 128)
    tags = region.reshape(2, 2, 2, 6, 2, 12).transpose(2, 4, 0, 1, 3, 5)[::-1, ::-1].reshape(8, SPAN)
    vmem = pl.BlockSpec(memory_space=pltpu.VMEM)
    dma = pltpu.SemaphoreType.DMA

    def pieces(dtype=BF16):
        return [pltpu.VMEM((n, D), dtype) for n in (224, 224, 96)]

    blended = pl.pallas_call(
        kernel,
        out_shape=jax.ShapeDtypeStruct((LEVELS * LEVEL, D), BF16),
        in_specs=[vmem] * 11,
        out_specs=vmem,
        scratch_shapes=[
            pltpu.VMEM((LEVELS * LEVEL, D), BF16),
            pltpu.VMEM((8, SPAN, D), BF16),
            pltpu.VMEM((6, 8, SPAN, 256), BF16),
            pltpu.VMEM((8, SPAN, D), BF16),
            pltpu.VMEM((LEVELS, LEVEL, D), F32),
            pltpu.VMEM((2, 16, 16, 16, 128), BF16),
            pltpu.VMEM((3 * D, D), BF16),
            pltpu.VMEM((D, D), BF16),
            *pieces(), *pieces(), *pieces(), *pieces(),
            dma((10,)), dma((11,)), dma((2, 16)), dma((2, 16)), dma((2, 16)), dma((2, 16)),
            dma((3,)), dma((3,)), dma((3,)), dma((3,)),
        ],
        compiler_params=pltpu.CompilerParams(
            collective_id=0, has_side_effects=True, vmem_limit_bytes=56 * 1024 * 1024
        ),
        name="attention_block",
    )(
        tokens.reshape(-1, D), tile, tags[:, None, :], tags[:, :, None], *constants()
    )
    return blended.reshape(tokens.shape)


def solution(mesh):
    placed = (P(None, "lat", "lon", None), P(None, "lat", "lon"), P("lat", "lon"), P("lat", "lon"))
    return jax.shard_map(
        local, mesh=mesh, in_specs=placed, out_specs=P(None, "lat", "lon", None), check_vma=False
    )
```

time: 326 us -> 75.4 us (0.23); the launches traced: 322 us -> 75.2 us
  blocking collectives: 173 us -> 0 us
  Pallas kernels: 0 us -> 68 us
  local copies, waits for them, and re-layouts: 47.5 us -> 6.42 us
  waiting for transfers between devices: 34.6 us -> 0 us
  matrix products: 33.8 us -> 0 us
  starting transfers between devices: 14.9 us -> 0 us
  between operations: 13.7 us -> 0.03 us
  other arithmetic: 4.41 us -> 0.7 us
    all_gather x3 -> x0, blocking collectives: 173 us -> none  [the longest x1 80.4 us: local(): lax.all_gather(qkv_weight, 'lon', axis=1, tiled=True)]
    pallas_call x0 -> x1, Pallas kernels: none -> 68 us  [local(): pl.pallas_call(kernel, out_shape=jax.ShapeDtypeStruct((LEVELS * LEVEL, D)...]
    dot_general x10 -> x0, matrix products: 20.8 us -> none  [the longest x8 15.2 us: one_head(): jnp.einsum('wqk,wkd->wqd', chances, value_rows, preferred_element_type=jn...]
    ppermute x4 -> x0, waiting for transfers between devices: 18.2 us -> none  [passed_along(): return lax.ppermute(block, axis, route)]
    all_gather x1 -> x0, waiting for transfers between devices: 16.4 us -> none  [local(): lax.all_gather(column_qkv, 'lat', axis=0, tiled=True)]
    ppermute x4 -> x0, starting transfers between devices: 14.9 us -> none  [passed_along(): return lax.ppermute(block, axis, route)]
    sub x8 -> x0, matrix products: 13.1 us -> none  [one_head(): raised = jnp.exp(scores - highest)]
    unnamed x12 -> x2, local copies, waits for them, and re-layouts: 15 us -> 3.16 us
  transfers between devices with their start and end apart: 5 -> 0, of which waited for: 4 -> 0; matrix products, arithmetic and copies ran while one was open for 1% -> 0% of each run, Pallas kernels for 0% -> 0%
where the time goes in v1:
time: 75.4 us; the launch traced here: 75.2 us
  Pallas kernels  68 us (90%)
  local copies, waits for them, and re-layouts  6.42 us (9%)
    pallas_call x1, Pallas kernels, local(): pl.pallas_call(kernel, out_shape=jax.ShapeDtypeStruct((LEVELS * LEVEL, D)...  68 us
    unnamed x2, local copies, waits for them, and re-layouts  3.16 us

profile of v1, /device:TPU:6, one launch (start us, length us, event | category | flops | bytes accessed | tf_op | source)
XLA Modules:
  0.0 75.2 jit_solution(5266601339201056761)
XLA Ops:
  0.0 0.8 %copy.15 = bf16[32,48]{0,1:T(8,128)(2,1)S(1)} copy(bf16[32,48]{1,0:T(8,128)(2,1)} %param.13) | data formatting | bytes 6144 | tf_op args[2]
  0.8 0.7 pad_maximum_fusion
  1.5 0.7 reshape.17.tile
  2.2 0.8 %reshape.18 = s32[2,2,2,6,2,12]{5,4,1,0,3,2:T(2,128)S(1)} reshape(s32[4,12,24]{2,0,1:T(4,128)} %param.12) | data formatting | bytes 9216 | tf_op jit(solution)/shard_map/reshape | solution.py:376
  3.0 0.7 broadcast_in_dim_reshape.8.tag_rows
  3.7 1.0 %broadcast_in_dim_reshape.9.tag_cols = s32[8,144,1]{2,1,0:T(8,128)} reshape(s32[2,2,2,2,6,12]{5,4,3,2,1,0:T(8,128)S(1)} %rev.3) | data formatting | bytes 9216 | tf_op jit(solution)/shard_map/broadcast_in_dim;reshape | solution.py:406
  4.8 68.0 %attention_block.1 = bf16[1152,512]{1,0:T(8,128)(2,1)} custom-call(bf16[1152,512]{1,0:T(8,128)(2,1)} %bitcast.13, bf16[16,128]{1,0:T(8,128)(2,1)} %reshape.17.tile, s32[8,1,144]{2,1,0:T(1,128)} %broadcast_in_dim_reshape.8.tag_rows, s32[8,144,1]{2,1,0:T(8,128)} %broadcast_in_dim_reshape.9.tag_cols, bf16[272,576]{1,0:T(8,128)(2,1)} %constant.14.clone.packs, ...), custom_call_target="tpu_custom_call" | custom-call | tf_op jit(solution)/shard_map/attention_block/pallas_call | solution.py:383
  72.8 2.4 %copy.23 = bf16[4,12,24,512]{3,2,1,0:T(8,128)(2,1)} copy(bf16[4,12,24,512]{3,2,1,0:T(8,128)(2,1)} %bitcast.12) | data formatting | bytes 2359296
  (3 shorter events, 0.0 us)

commit v2 on v1

v2 whole, which is shorter than its diff:
```python
import jax
import jax.numpy as jnp
import numpy as np
from jax import lax
from jax.experimental import pallas as pl
from jax.experimental.pallas import tpu as pltpu
from jax.sharding import PartitionSpec as P

MESH = pl.DeviceIdType.MESH
BF16 = jnp.bfloat16
F32 = jnp.float32

LEVELS, ROWS, COLS, D = 4, 12, 24, 512
HEADS = 8
LEVEL = ROWS * COLS
SPAN = 144
EPS = 1e-05
SCALE = float(np.log2(np.e) / 8.0)

RELATIVE = [0, 1, 2, 3, 4, -1, -2, -3, -4, 5, 6, 7, 8, -5, -6, -7]
PARTS = ((0, 9), (9, 7))


def positions(levels, rows, cols, pad=0):
    found = [(l, a, o) for l in levels for a in rows for o in cols]
    return found + [None] * pad


def one_hot(dest, source):
    where = {place: i for i, place in enumerate(source) if place is not None}
    matrix = np.zeros((len(dest), len(source)), np.float32)
    for i, place in enumerate(dest):
        if place in where:
            matrix[i, where[place]] = 1.0
    return matrix


BOTH = (0, 1)
OWN = positions(BOTH, range(ROWS), range(COLS))
W_PACK = positions(BOTH, range(3, 12), range(6), 4)
N_PACK = positions(BOTH, range(3), range(6, 24), 4)
C_PACK = positions(BOTH, range(3), range(6), 12)
E_SIDE = positions(BOTH, range(3, 12), range(24, 30), 4)
S_SIDE = positions(BOTH, range(12, 15), range(6, 24), 4)
C_SIDE = positions(BOTH, range(12, 15), range(24, 30), 12)
WINDOWS = [
    positions(BOTH, range(3 + 6 * i, 9 + 6 * i), range(6 + 12 * j, 18 + 12 * j))
    for j in (1, 0)
    for i in (1, 0)
]

PACKS = [one_hot(pack, OWN) for pack in (W_PACK, N_PACK, C_PACK)]
GATHERS = [one_hot(window, OWN) for window in WINDOWS]
SIDES = [
    [one_hot(WINDOWS[0], E_SIDE), one_hot(WINDOWS[0], S_SIDE), one_hot(WINDOWS[0], C_SIDE)],
    [one_hot(WINDOWS[1], E_SIDE), None, None],
    [None, one_hot(WINDOWS[2], S_SIDE), None],
    [None, None, None],
]


def lane_moves():
    moves = np.zeros((4, 128, 512), np.float32)
    for m in range(4):
        for q in range(4):
            for k in range(32):
                moves[m, q * 32 + k, q * 128 + m * 32 + k] = 1.0
    return moves


def tag_picks():
    rows = np.zeros((2, 2, SPAN, 12), np.float32)
    cols = np.zeros((2, SPAN, 24), np.float32)
    for n, (part, a, o) in enumerate(positions(BOTH, range(6), range(12))):
        for half in range(2):
            rows[half, part, n, 6 * half + a] = 1.0
            cols[half, n, 12 * half + o] = 1.0
    return rows, cols


SLABS = {0: (208, 80), 1: (64, 160), 2: (208, 80), 3: (64, 160)}


def own_level(pair, part):
    return (2 * pair + part + 1) % LEVELS


def nn(a, b):
    return lax.dot_general(a, b, (((1,), (0,)), ((), ())), preferred_element_type=F32)


def tn(a, b):
    return lax.dot_general(a, b, (((0,), (0,)), ((), ())), preferred_element_type=F32)


def nt(a, b):
    return lax.dot_general(a, b, (((1,), (1,)), ((), ())), preferred_element_type=F32)


def kernel(
    tokens_in, region_in, qkv_in, proj_in, packs_in, gathers_in, sides_in, moves_in, packs_t_in, gathers_t_in,
    sides_t_in, pick_rows_in, pick_cols_in,
    restored_out, proj_out,
    tokens, region, qkv_part, proj_part, packs, gathers, sides, moves, packs_t, gathers_t, sides_t, pick_rows, pick_cols,
    tag_rows, tag_cols, normed, windows, qkv, attended, restored, given, raw, whole_qkv, whole_proj,
    w_out, n_out, c_out, w_in, n_in, c_in, w_back, n_back, c_back, w_home, n_home, c_home,
    in_sem, out_sem,
    z_send, z_recv, p_send, p_recv, core_send, core_recv, halo_send, halo_recv, back_send, back_recv,
):
    lat = lax.axis_index("lat")
    lon = lax.axis_index("lon")
    core = lat % 2
    y = (lat // 2) % 4
    x = (lon % 2) * 2 + lat // 8
    z = lon // 2

    def at(xx, yy, zz, cc):
        return ((xx % 2) * 8 + yy * 2 + cc, zz * 2 + xx // 2)

    def along_z(step):
        return at(x, y, (z + step + 16) % 16, core)

    def one_way(d):
        return at((x + d * (1 - core)) % 4, (y + d * core) % 4, z, core)

    def other_way(d):
        return at((x + d * core) % 4, (y + d * (1 - core)) % 4, z, core)

    def beside(d_lat, d_lon):
        return ((lat + d_lat + 16) % 16, (lon + d_lon + 32) % 32)

    peer = at(x, y, z, 1 - core)
    near = [s for s in RELATIVE if 0 < abs(s) <= 4]
    partners = [along_z(s) for s in near]
    partners += [one_way(d) for d in (1, 2, 3)] + [other_way(d) for d in (1, 2, 3)] + [peer]
    partners += [beside(a, b) for a, b in ((0, 1), (0, -1), (1, 0), (-1, 0), (1, 1), (-1, -1))]
    barrier = pltpu.get_barrier_semaphore()
    for partner in partners:
        pl.semaphore_signal(barrier, 1, device_id=partner, device_id_type=MESH)

    loads = [
        pltpu.make_async_copy(src, dst, in_sem.at[n])
        for n, (src, dst) in enumerate((
            (qkv_in, qkv_part), (proj_in, proj_part), (tokens_in, tokens), (packs_in, packs), (region_in, region),
            (pick_rows_in, pick_rows), (pick_cols_in, pick_cols), (gathers_in, gathers), (sides_in, sides),
            (moves_in, moves), (sides_t_in, sides_t), (gathers_t_in, gathers_t), (packs_t_in, packs_t),
        ))
    ]
    for load in loads:
        load.start()

    loads[0].wait()
    loads[1].wait()
    line = lax.broadcasted_iota(jnp.int32, (32, 128), 0)
    lane = lax.broadcasted_iota(jnp.int32, (32, 128), 1)
    total = 0.0
    for q in range(4):
        place = jnp.where(lane == line + 32 * q, 1.0, 0.0).astype(BF16)
        if q < 3:
            total += tn(qkv_part[...], place)[q * 16:(q + 1) * 16]
        else:
            total += tn(proj_part[...], place)
    raw[0, 0, 0, 0] = total.astype(BF16)

    loads[2].wait()

    @pl.loop(0, LEVELS)
    def _(i):
        rows = pl.ds(pl.multiple_of(i * LEVEL, LEVEL), LEVEL)
        floated = tokens[rows, :].astype(F32)
        average = jnp.mean(floated, axis=-1, keepdims=True)
        centred = floated - average
        spread = jnp.mean(centred * centred, axis=-1, keepdims=True)
        normed[rows, :] = (centred * lax.rsqrt(spread + EPS)).astype(BF16)

    def slab(pair, part, start, size):
        return normed[pl.ds(own_level(pair, part) * LEVEL + start, size), :]

    loads[3].wait()
    for pair in range(2):
        for buf, first, size, start, height in (
            (w_out, 0, 112, 64, 224), (n_out, 112, 112, 0, 80), (c_out, 224, 48, 0, 80),
        ):
            total = 0.0
            for part in range(2):
                chosen = packs[pl.ds(first, size), pl.ds(part * LEVEL, LEVEL)][:, start:start + height]
                total += nn(chosen, slab(pair, part, start, height))
            buf[pl.ds(pair * size, size), :] = total.astype(BF16)

    pl.semaphore_wait(barrier, len(partners))

    def remote(src, dst, send, recv, target):
        return pltpu.make_async_remote_copy(src, dst, send, recv, device_id=target, device_id_type=MESH)

    first = []
    for n, s in enumerate(near):
        slot = RELATIVE.index(-s)
        copy = remote(raw.at[0, 0, 0, 0], raw.at[0, 0, 0, slot], z_send.at[n], z_recv.at[slot], along_z(s))
        copy.start()
        first.append(copy)
    halos = []
    for n, (src, dst, target) in enumerate((
        (w_out, w_in, beside(0, -1)), (c_out, c_in, beside(-1, -1)), (n_out, n_in, beside(-1, 0)),
    )):
        copy = remote(src, dst, halo_send.at[n], halo_recv.at[n], target)
        copy.start()
        halos.append(copy)
    for copy in first:
        copy.wait_recv()

    far = [
        remote(raw.at[0, 0, 0, pl.ds(1, 4)], raw.at[0, 0, 0, pl.ds(9, 4)], z_send.at[8], z_recv.at[9], along_z(-4)),
        remote(raw.at[0, 0, 0, pl.ds(5, 3)], raw.at[0, 0, 0, pl.ds(13, 3)], z_send.at[9], z_recv.at[10], along_z(4)),
    ]
    for copy in far:
        copy.start()

    def step_one(part, d):
        span = pl.ds(*PARTS[part])
        return remote(
            raw.at[0, 0, 0, span], raw.at[0, 4 - d, 0, span], p_send.at[part, d, 0], p_recv.at[part, 4 - d, 0], one_way(d)
        )

    def step_two(part, i, d):
        span = pl.ds(*PARTS[part])
        return remote(
            raw.at[0, i, 0, span], raw.at[0, i, 4 - d, span], p_send.at[part, i, d], p_recv.at[part, i, 4 - d], other_way(d)
        )

    def arrival(part, i, k):
        span = pl.ds(*PARTS[part])
        return remote(
            raw.at[0, 0, 0, span], raw.at[0, i, k, span], p_send.at[part, i, k], p_recv.at[part, i, k], peer
        )

    def relay(part, i, k):
        span = pl.ds(*PARTS[part])
        return remote(
            raw.at[0, i, k, span], raw.at[1, i, k, span], core_send.at[part, i, k], core_recv.at[part, i, k], peer
        )

    def begin(part):
        for d in (1, 3, 2):
            step_one(part, d).start()
        for d in (1, 3, 2):
            step_two(part, 0, d).start()
        relay(part, 0, 0).start()

    def forward(part):
        for i in (1, 3, 2):
            arrival(part, i, 0).wait_recv()
            for d in (1, 3, 2):
                step_two(part, i, d).start()
            relay(part, i, 0).start()

    begin(0)
    forward(0)
    for copy in far:
        copy.wait_recv()
    begin(1)
    forward(1)
    for part in range(2):

        @pl.loop(0, 4)
        def _(i):
            for k in (1, 3, 2):
                arrival(part, i, k).wait_recv()
                relay(part, i, k).start()

    for n in (4, 5, 6, 7, 8):
        loads[n].wait()
    for w in range(4):
        half_lat, half_lon = (1, 0, 1, 0)[w], (1, 1, 0, 0)[w]
        for pair in range(2):
            column = 0.0
            for part in range(2):
                ids = region[2 * pair + part].astype(F32).astype(BF16)
                column += nn(pick_rows[half_lat, part], ids)
            column = jnp.sum(column * pick_cols[half_lon].astype(F32), axis=-1, keepdims=True)
            square = (SPAN, SPAN)
            same = lax.broadcasted_iota(jnp.int32, square, 0) == lax.broadcasted_iota(jnp.int32, square, 1)
            spots = jnp.where(same, column, 0.0).astype(BF16)
            tag_cols[2 * w + pair] = column
            tag_rows[2 * w + pair] = nn(jnp.ones((8, SPAN), BF16), spots)

    for copy in halos:
        copy.wait_recv()
    beginnings = (0, 112, 224)
    sizes = (112, 112, 48)
    for pair in range(2):
        for w in range(4):
            start, height = SLABS[w]
            total = 0.0
            for part in range(2):
                chosen = gathers[w, :, pl.ds(part * LEVEL, LEVEL)][:, start:start + height]
                total += nn(chosen, slab(pair, part, start, height))
            for k, arrived in enumerate((w_in, n_in, c_in)):
                if SIDES[w][k] is not None:
                    total += nn(
                        sides[w, :, pl.ds(k * 128, sizes[k])], arrived[pl.ds(pair * sizes[k], sizes[k]), :]
                    )
            windows[pl.ds((2 * w + pair) * SPAN, SPAN), :] = total.astype(BF16)

    for part in range(2):

        @pl.loop(0, 4)
        def _(i):
            for k in range(4):
                relay(part, i, k).wait_recv()

    loads[9].wait()
    for x_hi in range(2):
        for group in range(4):
            x_lo, y_hi = group // 2, group % 2
            total = 0.0
            for member in range(4):
                y_lo, cc = member // 2, member % 2
                d_x, d_y = (x_hi * 2 + x_lo - x + 4) % 4, (y_hi * 2 + y_lo - y + 4) % 4
                i, k = (d_x, d_y) if cc == 0 else (d_y, d_x)
                piece = raw[(cc + core) % 2, i, k].reshape(256, 128)
                total += nn(piece, moves[member])
            total = total.astype(BF16)
            lanes = pl.ds(group * 128, 128)
            for s in range(16):
                band = ((z + RELATIVE[s] + 16) % 16) * 2 + x_hi
                for q in range(4):
                    block = total[s * 16:(s + 1) * 16, q * 128:(q + 1) * 128]
                    if q < 3:
                        whole_qkv[pl.ds(pl.multiple_of(band * 48 + q * 16, 16), 16), lanes] = block
                    else:
                        whole_proj[pl.ds(pl.multiple_of(band * 16, 16), 16), lanes] = block

    proj_copy = pltpu.make_async_copy(whole_proj, proj_out, out_sem.at[4])
    proj_copy.start()

    def project_in(half):
        rows = pl.ds(half * 4 * SPAN, 4 * SPAN)
        for n in range(6):
            qkv[n, rows, :] = nt(windows[rows, :], whole_qkv[pl.ds(n * 256, 256), :]).astype(BF16)

    lower = lax.broadcasted_iota(jnp.int32, (SPAN, 128), 1) < 64
    ones = jnp.ones((SPAN, 128), BF16)

    def attend(w):
        rows = pl.ds(pl.multiple_of(w * SPAN, 16), SPAN)
        bias = jnp.where(tag_cols[w] == tag_rows[w][0:1], 0.0, -1e30)
        bias = jnp.concatenate([bias, bias], axis=0)
        scores = []
        for t in range(4):
            lanes = slice((t % 2) * 128, (t % 2) * 128 + 128)
            query = qkv[t // 2, rows, lanes]
            zero = jnp.zeros_like(query)
            both = jnp.concatenate([jnp.where(lower, query, zero), jnp.where(lower, zero, query)], axis=0)
            scores.append(nt(both, qkv[2 + t // 2, rows, lanes]) + bias)
        raised = [
            jnp.exp2((score - jnp.max(score, axis=-1, keepdims=True)) * SCALE).astype(BF16) for score in scores
        ]
        for t in range(4):
            lanes = slice((t % 2) * 128, (t % 2) * 128 + 128)
            mixed = nn(raised[t], jnp.concatenate([qkv[4 + t // 2, rows, lanes], ones], axis=1))
            top = jnp.where(lower, mixed[:SPAN, :128], mixed[SPAN:, :128])
            bottom = jnp.where(lower, mixed[:SPAN, 128:], mixed[SPAN:, 128:])
            attended[w, :, pl.ds(t * 128, 128)] = (top / bottom).astype(BF16)

    def give_back(k, buf, sources, pair):
        total = 0.0
        for w in sources:
            total += nn(sides_t[w, pl.ds(k * 128, sizes[k]), :], attended[2 * w + pair])
        buf[pl.ds(pair * sizes[k], sizes[k]), :] = total.astype(BF16)

    returns = []

    def send_back(k, src, dst, target):
        copy = remote(src, dst, back_send.at[k], back_recv.at[k], target)
        copy.start()
        returns.append(copy)

    project_in(0)

    @pl.loop(0, 2)
    def _(w):
        attend(w)

    loads[10].wait()
    for pair in range(2):
        give_back(2, c_back, (0,), pair)
    send_back(2, c_back, c_home, beside(1, 1))

    @pl.loop(2, 4)
    def _(w):
        attend(w)

    for pair in range(2):
        give_back(0, w_back, (0, 1), pair)
    send_back(0, w_back, w_home, beside(0, 1))

    project_in(1)

    @pl.loop(4, 6)
    def _(w):
        attend(w)

    for pair in range(2):
        give_back(1, n_back, (0, 2), pair)
    send_back(1, n_back, n_home, beside(1, 0))

    @pl.loop(6, 8)
    def _(w):
        attend(w)

    loads[11].wait()
    for pair in range(2):
        for part in range(2):
            total = 0.0
            for w in range(4):
                total += nn(gathers_t[w, pl.ds(part * LEVEL, LEVEL), :], attended[2 * w + pair])
            restored[own_level(pair, part)] = total

    loads[12].wait()
    for copy in returns:
        copy.wait_recv()
    written = [proj_copy]
    for pair in range(2):
        for part in range(2):
            level = own_level(pair, part)
            total = restored[level]
            for k, home in enumerate((w_home, n_home, c_home)):
                total += nn(
                    packs_t[pl.ds(part * LEVEL, LEVEL), pl.ds(k * 128, sizes[k])],
                    home[pl.ds(pair * sizes[k], sizes[k]), :],
                )
            rows = pl.ds(level * LEVEL, LEVEL)
            given[rows, :] = total.astype(BF16)
            copy = pltpu.make_async_copy(given.at[rows, :], restored_out.at[rows, :], out_sem.at[level])
            copy.start()
            written.append(copy)

    for copy in first + far + halos + returns:
        copy.wait_send()
    for part in range(2):
        for d in (1, 2, 3):
            step_one(part, d).wait_send()

        @pl.loop(0, 4)
        def _(i):
            for d in (1, 2, 3):
                step_two(part, i, d).wait_send()
            for k in range(4):
                relay(part, i, k).wait_send()

    for copy in written:
        copy.wait()


def constants():
    packs = np.concatenate(PACKS, axis=0)
    gathers = np.stack(GATHERS)
    sides = np.zeros((3, SPAN, 384), np.float32)
    for w in range(3):
        for k, matrix in enumerate(SIDES[w]):
            if matrix is not None:
                sides[w, :, k * 128:k * 128 + matrix.shape[1]] = matrix
    packs_t = np.zeros((2 * LEVEL, 384), np.float32)
    for k, matrix in enumerate(PACKS):
        packs_t[:, k * 128:k * 128 + matrix.shape[0]] = matrix.T
    pick_rows, pick_cols = tag_picks()
    return [
        jnp.asarray(a, BF16)
        for a in (
            packs, gathers, sides, lane_moves(), packs_t, gathers.transpose(0, 2, 1), sides.transpose(0, 2, 1),
            pick_rows, pick_cols,
        )
    ]


def local(tokens, region, qkv_weight, proj_weight):
    flat = tokens.reshape(-1, D)
    operands = [flat, region, qkv_weight, proj_weight, *constants()]
    anywhere = pl.BlockSpec(memory_space=pl.ANY)
    dma = pltpu.SemaphoreType.DMA

    def pieces():
        return [pltpu.VMEM((n, D), BF16) for n in (224, 224, 96)]

    restored, whole_proj = pl.pallas_call(
        kernel,
        out_shape=[jax.ShapeDtypeStruct(flat.shape, BF16), jax.ShapeDtypeStruct((D, D), BF16)],
        in_specs=[anywhere] * len(operands),
        out_specs=[anywhere] * 2,
        scratch_shapes=[
            *[pltpu.VMEM(a.shape, a.dtype) for a in operands],
            pltpu.VMEM((8, 8, SPAN), F32),
            pltpu.VMEM((8, SPAN, 1), F32),
            pltpu.VMEM((LEVELS * LEVEL, D), BF16),
            pltpu.VMEM((8 * SPAN, D), BF16),
            pltpu.VMEM((6, 8 * SPAN, 256), BF16),
            pltpu.VMEM((8, SPAN, D), BF16),
            pltpu.VMEM((LEVELS, LEVEL, D), F32),
            pltpu.VMEM((LEVELS * LEVEL, D), BF16),
            pltpu.VMEM((2, 4, 4, 16, 16, 128), BF16),
            pltpu.VMEM((3 * D, D), BF16),
            pltpu.VMEM((D, D), BF16),
            *pieces(), *pieces(), *pieces(), *pieces(),
            dma((len(operands),)), dma((5,)),
            dma((10,)), dma((11,)), dma((2, 4, 4)), dma((2, 4, 4)), dma((2, 4, 4)), dma((2, 4, 4)),
            dma((3,)), dma((3,)), dma((3,)), dma((3,)),
        ],
        compiler_params=pltpu.CompilerParams(
            collective_id=0, has_side_effects=True, vmem_limit_bytes=56 * 1024 * 1024
        ),
        name="attention_block",
    )(*operands)
    blended = flat.astype(F32) + nt(restored, whole_proj)
    return blended.astype(BF16).reshape(tokens.shape)


def solution(mesh):
    placed = (P(None, "lat", "lon", None), P(None, "lat", "lon"), P("lat", "lon"), P("lat", "lon"))
    return jax.shard_map(
        local, mesh=mesh, in_specs=placed, out_specs=P(None, "lat", "lon", None), check_vma=False
    )
```

time: 75.4 us -> 65.3 us (0.87); the launches traced: 75.2 us -> 64.3 us
  Pallas kernels: 68 us -> 58.3 us
  local copies, waits for them, and re-layouts: 6.42 us -> 2.71 us
  matrix products: 0 us -> 3.22 us
    pallas_call x1, Pallas kernels: 68 us -> 58.3 us  [local(): pl.pallas_call(kernel, out_shape=[jax.ShapeDtypeStruct(flat.shape, BF16),...]
    dot_general x0 -> x1, matrix products: none -> 3.22 us  [nt(): lax.dot_general(a, b, (((1,), (1,)), ((), ())), preferred_element_type=F32)]
    another operation x2 -> x0, local copies, waits for them, and re-layouts: 1.71 us -> none  [the longest x1 1.02 us: local(): tags[:, :, None]]
    reshape x3 -> x0, local copies, waits for them, and re-layouts: 1.53 us -> none  [the longest x2 0.85 us: local(): region.reshape(2, 2, 2, 6, 2, 12).transpose(2, 4, 0, 1, 3, 5)[::-1, ::-1]]
    unnamed x2 -> x4, local copies, waits for them, and re-layouts: 3.16 us -> 2.71 us
where the time goes in v2:
time: 65.3 us; the launch traced here: 64.3 us
  Pallas kernels  58.3 us (89%)
  matrix products  3.22 us (5%)
  local copies, waits for them, and re-layouts  2.71 us (4%)
    pallas_call x1, Pallas kernels, local(): pl.pallas_call(kernel, out_shape=[jax.ShapeDtypeStruct(flat.shape, BF16),...  58.3 us
    dot_general x1, matrix products, nt(): lax.dot_general(a, b, (((1,), (1,)), ((), ())), preferred_element_type=F32)  3.22 us
    unnamed x4, local copies, waits for them, and re-layouts  2.71 us

profile of v2, /device:TPU:6, one launch (start us, length us, event | category | flops | bytes accessed | tf_op | source)
XLA Modules:
  0.0 64.3 jit_solution(6442320815950130955)
XLA Ops:
  0.0 1.4 %copy.15.proj_in = bf16[32,16]{1,0:T(8,128)(2,1)} copy(bf16[32,16]{0,1:T(8,128)(2,1)} %param.16) | data formatting | bytes 2048 | tf_op args[3]
  1.4 1.4 %copy.14.region_in = s32[4,12,24]{2,1,0:T(8,128)} copy(s32[4,12,24]{2,0,1:T(4,128)} %param.14) | data formatting | bytes 9216 | tf_op args[1]
  2.7 0.0 copy-start
  2.7 58.3 %attention_block.1 = (bf16[1152,512]{1,0:T(8,128)(2,1)}, bf16[512,512]{1,0:T(8,128)(2,1)}) custom-call(bf16[1152,512]{1,0:T(8,128)(2,1)} %bitcast.4, s32[4,12,24]{2,1,0:T(8,128)} %copy.14.region_in, bf16[32,48]{1,0:T(8,128)(2,1)} %qkv_in.1, bf16[32,16]{1,0:T(8,128)(2,1)} %copy.15.proj_in, bf16[272,576]{1,0:T(8,128)(2,1)} %constant.18.clone.packs_in, ...), custom_call_target="tpu_custom_call" | custom-call | tf_op jit(solution)/shard_map/attention_block/pallas_call | solution.py:485
  61.1 0.0 copy-done
  61.1 3.2 %fusion = bf16[1152,512]{1,0:T(8,128)(2,1)} fusion(bf16[1152,512]{1,0:T(8,128)(2,1)} %get-tuple-element.7, bf16[512,512]{1,0:T(8,128)(2,1)} %get-tuple-element.8, bf16[1152,512]{1,0:T(8,128)(2,1)S(1)} %bitcast.5), kind=kOutput, calls=%fused_computation.1 | convolution fusion | flops 605749248 | bytes 4063232 | tf_op jit(solution)/shard_map/dot_general | solution.py:97
Async XLA Ops:
  2.7 58.4 %copy-start = (bf16[4,12,24,512]{3,2,1,0:T(8,128)(2,1)S(1)}, bf16[4,12,24,512]{3,2,1,0:T(8,128)(2,1)}, u32[]{:S(2)}) copy-start(bf16[4,12,24,512]{3,2,1,0:T(8,128)(2,1)} %param.13) | copy-start | bytes 3538948

commit v3 on v2

--- a/solution.py
+++ b/solution.py
@@ -69,16 +69,21 @@
 
 
 def tag_picks():
-    rows = np.zeros((2, 2, SPAN, 12), np.float32)
-    cols = np.zeros((2, SPAN, 24), np.float32)
+    rows = np.zeros((2, 2, SPAN, ROWS * LEVELS), np.float32)
+    cols = np.zeros((2, SPAN, COLS), np.float32)
     for n, (part, a, o) in enumerate(positions(BOTH, range(6), range(12))):
         for half in range(2):
-            rows[half, part, n, 6 * half + a] = 1.0
             cols[half, n, 12 * half + o] = 1.0
+            for pair in range(2):
+                rows[half, pair, n, (6 * half + a) * LEVELS + 2 * pair + part] = 1.0
     return rows, cols
 
 
 SLABS = {0: (208, 80), 1: (64, 160), 2: (208, 80), 3: (64, 160)}
+
+
+def place(w, pair):
+    return pair * 2 + w if w < 2 else w * 2 + pair
 
 
 def own_level(pair, part):
@@ -102,7 +107,7 @@
     sides_t_in, pick_rows_in, pick_cols_in,
     restored_out, proj_out,
     tokens, region, qkv_part, proj_part, packs, gathers, sides, moves, packs_t, gathers_t, sides_t, pick_rows, pick_cols,
-    tag_rows, tag_cols, normed, windows, qkv, attended, restored, given, raw, whole_qkv, whole_proj,
+    ids, tag_rows, tag_cols, normed, windows, qkv, attended, restored, given, raw, whole_qkv, whole_proj,
     w_out, n_out, c_out, w_in, n_in, c_in, w_back, n_back, c_back, w_home, n_home, c_home,
     in_sem, out_sem,
     z_send, z_recv, p_send, p_recv, core_send, core_recv, halo_send, halo_recv, back_send, back_recv,
@@ -121,10 +126,10 @@
         return at(x, y, (z + step + 16) % 16, core)
 
     def one_way(d):
-        return at((x + d * (1 - core)) % 4, (y + d * core) % 4, z, core)
+        return at((x + d) % 4, y, z, core)
 
     def other_way(d):
-        return at((x + d * core) % 4, (y + d * (1 - core)) % 4, z, core)
+        return at(x, (y + d) % 4, z, core)
 
     def beside(d_lat, d_lon):
         return ((lat + d_lat + 16) % 16, (lon + d_lon + 32) % 32)
@@ -155,13 +160,24 @@
     lane = lax.broadcasted_iota(jnp.int32, (32, 128), 1)
     total = 0.0
     for q in range(4):
-        place = jnp.where(lane == line + 32 * q, 1.0, 0.0).astype(BF16)
+        spot = jnp.where(lane == line + 32 * q, 1.0, 0.0).astype(BF16)
         if q < 3:
-            total += tn(qkv_part[...], place)[q * 16:(q + 1) * 16]
+            total += tn(qkv_part[...], spot)[q * 16:(q + 1) * 16]
         else:
-            total += tn(proj_part[...], place)
+            total += nn(proj_part[...], spot)
     raw[0, 0, 0, 0] = total.astype(BF16)
 
+    pl.semaphore_wait(barrier, len(partners))
+
+    def remote(src, dst, send, recv, target):
+        return pltpu.make_async_remote_copy(src, dst, send, recv, device_id=target, device_id_type=MESH)
+
+    first = []
+    for n, s in enumerate(near):
+        slot = RELATIVE.index(-s)
+        copy = remote(raw.at[0, 0, 0, 0], raw.at[0, 0, 0, slot], z_send.at[n], z_recv.at[slot], along_z(s))
+        copy.start()
+        first.append(copy)
     loads[2].wait()
 
     @pl.loop(0, LEVELS)
@@ -178,33 +194,30 @@
 
     loads[3].wait()
     for pair in range(2):
-        for buf, first, size, start, height in (
+        for buf, begins, size, start, height in (
             (w_out, 0, 112, 64, 224), (n_out, 112, 112, 0, 80), (c_out, 224, 48, 0, 80),
         ):
             total = 0.0
             for part in range(2):
-                chosen = packs[pl.ds(first, size), pl.ds(part * LEVEL, LEVEL)][:, start:start + height]
+                chosen = packs[pl.ds(begins, size), pl.ds(part * LEVEL, LEVEL)][:, start:start + height]
                 total += nn(chosen, slab(pair, part, start, height))
             buf[pl.ds(pair * size, size), :] = total.astype(BF16)
 
-    pl.semaphore_wait(barrier, len(partners))
-
-    def remote(src, dst, send, recv, target):
-        return pltpu.make_async_remote_copy(src, dst, send, recv, device_id=target, device_id_type=MESH)
-
-    first = []
-    for n, s in enumerate(near):
-        slot = RELATIVE.index(-s)
-        copy = remote(raw.at[0, 0, 0, 0], raw.at[0, 0, 0, slot], z_send.at[n], z_recv.at[slot], along_z(s))
-        copy.start()
-        first.append(copy)
     halos = []
-    for n, (src, dst, target) in enumerate((
-        (w_out, w_in, beside(0, -1)), (c_out, c_in, beside(-1, -1)), (n_out, n_in, beside(-1, 0)),
-    )):
-        copy = remote(src, dst, halo_send.at[n], halo_recv.at[n], target)
+
+    def send_halo(n, pair):
+        src, dst, size, target = (
+            (w_out, w_in, 112, beside(0, -1)), (n_out, n_in, 112, beside(-1, 0)), (c_out, c_in, 48, beside(-1, -1)),
+        )[n]
+        rows = pl.ds(pair * size, size)
+        copy = remote(src.at[rows, :], dst.at[rows, :], halo_send.at[n, pair], halo_recv.at[n, pair], target)
         copy.start()
         halos.append(copy)
+
+    send_halo(0, 0)
+    send_halo(2, 0)
+    send_halo(1, 0)
+    send_halo(1, 1)
     for copy in first:
         copy.wait_recv()
 
@@ -253,39 +266,71 @@
                 step_two(part, i, d).start()
             relay(part, i, 0).start()
 
+    def pass_on(part, i):
+        for k in (1, 3, 2):
+            arrival(part, i, k).wait_recv()
+            relay(part, i, k).start()
+
+    def unpack(part):
+        @pl.loop(0, 4)
+        def _(i):
+            for k in range(4):
+                relay(part, i, k).wait_recv()
+
+        start, count = PARTS[part]
+        for x_hi in range(2):
+            for group in range(4):
+                x_lo, y_hi = group // 2, group % 2
+                total = 0.0
+                for member in range(4):
+                    y_lo, cc = member // 2, member % 2
+                    d_x, d_y = (x_hi * 2 + x_lo - x + 4) % 4, (y_hi * 2 + y_lo - y + 4) % 4
+                    piece = raw[(cc + core) % 2, d_x, d_y, pl.ds(start, count)].reshape(count * 16, 128)
+                    total += nn(piece, moves[member])
+                total = total.astype(BF16)
+                lanes = pl.ds(group * 128, 128)
+                for s in range(count):
+                    band = ((z + RELATIVE[start + s] + 16) % 16) * 2 + x_hi
+                    for q in range(4):
+                        block = total[s * 16:(s + 1) * 16, q * 128:(q + 1) * 128]
+                        if q < 3:
+                            whole_qkv[pl.ds(pl.multiple_of(band * 48 + q * 16, 16), 16), lanes] = block
+                        else:
+                            whole_proj[pl.ds(pl.multiple_of(band * 16, 16), 16), lanes] = block
+
     begin(0)
+    for n in (4, 5, 6):
+        loads[n].wait()
+    for a in range(ROWS):
+        ids[pl.ds(a * LEVELS, LEVELS), :] = region[a].astype(F32)
+    for w in range(4):
+        half_lat, half_lon = (1, 0, 1, 0)[w], (1, 1, 0, 0)[w]
+        for pair in range(2):
+            column = nn(pick_rows[half_lat, pair], ids[...].astype(BF16))
+            column = jnp.sum(column * pick_cols[half_lon].astype(F32), axis=-1, keepdims=True)
+            square = (SPAN, SPAN)
+            same = lax.broadcasted_iota(jnp.int32, square, 0) == lax.broadcasted_iota(jnp.int32, square, 1)
+            spots = jnp.where(same, column, 0.0).astype(BF16)
+            tag_cols[place(w, pair)] = column
+            tag_rows[place(w, pair)] = nn(jnp.ones((8, SPAN), BF16), spots)
+
     forward(0)
     for copy in far:
         copy.wait_recv()
     begin(1)
+    send_halo(0, 1)
+    send_halo(2, 1)
+    pass_on(0, 0)
     forward(1)
-    for part in range(2):
-
-        @pl.loop(0, 4)
-        def _(i):
-            for k in (1, 3, 2):
-                arrival(part, i, k).wait_recv()
-                relay(part, i, k).start()
-
-    for n in (4, 5, 6, 7, 8):
-        loads[n].wait()
-    for w in range(4):
-        half_lat, half_lon = (1, 0, 1, 0)[w], (1, 1, 0, 0)[w]
-        for pair in range(2):
-            column = 0.0
-            for part in range(2):
-                ids = region[2 * pair + part].astype(F32).astype(BF16)
-                column += nn(pick_rows[half_lat, part], ids)
-            column = jnp.sum(column * pick_cols[half_lon].astype(F32), axis=-1, keepdims=True)
-            square = (SPAN, SPAN)
-            same = lax.broadcasted_iota(jnp.int32, square, 0) == lax.broadcasted_iota(jnp.int32, square, 1)
-            spots = jnp.where(same, column, 0.0).astype(BF16)
-            tag_cols[2 * w + pair] = column
-            tag_rows[2 * w + pair] = nn(jnp.ones((8, SPAN), BF16), spots)
-
+
+    @pl.loop(1, 4)
+    def _(i):
+        pass_on(0, i)
+
+    loads[7].wait()
+    loads[8].wait()
     for copy in halos:
         copy.wait_recv()
-    beginnings = (0, 112, 224)
     sizes = (112, 112, 48)
     for pair in range(2):
         for w in range(4):
@@ -299,42 +344,22 @@
                     total += nn(
                         sides[w, :, pl.ds(k * 128, sizes[k])], arrived[pl.ds(pair * sizes[k], sizes[k]), :]
                     )
-            windows[pl.ds((2 * w + pair) * SPAN, SPAN), :] = total.astype(BF16)
-
-    for part in range(2):
-
-        @pl.loop(0, 4)
-        def _(i):
-            for k in range(4):
-                relay(part, i, k).wait_recv()
-
+            windows[pl.ds(place(w, pair) * SPAN, SPAN), :] = total.astype(BF16)
+
+    pass_on(1, 0)
     loads[9].wait()
-    for x_hi in range(2):
-        for group in range(4):
-            x_lo, y_hi = group // 2, group % 2
-            total = 0.0
-            for member in range(4):
-                y_lo, cc = member // 2, member % 2
-                d_x, d_y = (x_hi * 2 + x_lo - x + 4) % 4, (y_hi * 2 + y_lo - y + 4) % 4
-                i, k = (d_x, d_y) if cc == 0 else (d_y, d_x)
-                piece = raw[(cc + core) % 2, i, k].reshape(256, 128)
-                total += nn(piece, moves[member])
-            total = total.astype(BF16)
-            lanes = pl.ds(group * 128, 128)
-            for s in range(16):
-                band = ((z + RELATIVE[s] + 16) % 16) * 2 + x_hi
-                for q in range(4):
-                    block = total[s * 16:(s + 1) * 16, q * 128:(q + 1) * 128]
-                    if q < 3:
-                        whole_qkv[pl.ds(pl.multiple_of(band * 48 + q * 16, 16), 16), lanes] = block
-                    else:
-                        whole_proj[pl.ds(pl.multiple_of(band * 16, 16), 16), lanes] = block
-
+    unpack(0)
+
+    @pl.loop(1, 4)
+    def _(i):
+        pass_on(1, i)
+
+    unpack(1)
     proj_copy = pltpu.make_async_copy(whole_proj, proj_out, out_sem.at[4])
     proj_copy.start()
 
-    def project_in(half):
-        rows = pl.ds(half * 4 * SPAN, 4 * SPAN)
+    def project_in(start, count):
+        rows = pl.ds(start * SPAN, count * SPAN)
         for n in range(6):
             qkv[n, rows, :] = nt(windows[rows, :], whole_qkv[pl.ds(n * 256, 256), :]).astype(BF16)
 
@@ -362,47 +387,38 @@
             bottom = jnp.where(lower, mixed[:SPAN, 128:], mixed[SPAN:, 128:])
             attended[w, :, pl.ds(t * 128, 128)] = (top / bottom).astype(BF16)
 
-    def give_back(k, buf, sources, pair):
+    returns = []
+
+    def give_back(k, sources, pair, target):
         total = 0.0
         for w in sources:
-            total += nn(sides_t[w, pl.ds(k * 128, sizes[k]), :], attended[2 * w + pair])
-        buf[pl.ds(pair * sizes[k], sizes[k]), :] = total.astype(BF16)
-
-    returns = []
-
-    def send_back(k, src, dst, target):
-        copy = remote(src, dst, back_send.at[k], back_recv.at[k], target)
+            total += nn(sides_t[w, pl.ds(k * 128, sizes[k]), :], attended[place(w, pair)])
+        rows = pl.ds(pair * sizes[k], sizes[k])
+        src, dst = ((w_back, w_home), (n_back, n_home), (c_back, c_home))[k]
+        src[rows, :] = total.astype(BF16)
+        copy = remote(src.at[rows, :], dst.at[rows, :], back_send.at[k, pair], back_recv.at[k, pair], target)
         copy.start()
         returns.append(copy)
 
-    project_in(0)
-
-    @pl.loop(0, 2)
-    def _(w):
-        attend(w)
-
     loads[10].wait()
     for pair in range(2):
-        give_back(2, c_back, (0,), pair)
-    send_back(2, c_back, c_home, beside(1, 1))
-
-    @pl.loop(2, 4)
-    def _(w):
-        attend(w)
-
-    for pair in range(2):
-        give_back(0, w_back, (0, 1), pair)
-    send_back(0, w_back, w_home, beside(0, 1))
-
-    project_in(1)
+        project_in(2 * pair, 2)
+
+        @pl.loop(2 * pair, 2 * pair + 2)
+        def _(w):
+            attend(w)
+
+        give_back(0, (0, 1), pair, beside(0, 1))
+        give_back(2, (0,), pair, beside(1, 1))
+
+    project_in(4, 4)
 
     @pl.loop(4, 6)
     def _(w):
         attend(w)
 
     for pair in range(2):
-        give_back(1, n_back, (0, 2), pair)
-    send_back(1, n_back, n_home, beside(1, 0))
+        give_back(1, (0, 2), pair, beside(1, 0))
 
     @pl.loop(6, 8)
     def _(w):
@@ -413,7 +429,7 @@
         for part in range(2):
             total = 0.0
             for w in range(4):
-                total += nn(gathers_t[w, pl.ds(part * LEVEL, LEVEL), :], attended[2 * w + pair])
+                total += nn(gathers_t[w, pl.ds(part * LEVEL, LEVEL), :], attended[place(w, pair)])
             restored[own_level(pair, part)] = total
 
     loads[12].wait()
@@ -475,7 +491,8 @@
 
 def local(tokens, region, qkv_weight, proj_weight):
     flat = tokens.reshape(-1, D)
-    operands = [flat, region, qkv_weight, proj_weight, *constants()]
+    operands = [flat, region.transpose(1, 0, 2), qkv_weight, proj_weight.T, *constants()]
+    operands = [pltpu.with_memory_space_constraint(a, pltpu.HBM) for a in operands]
     anywhere = pl.BlockSpec(memory_space=pl.ANY)
     dma = pltpu.SemaphoreType.DMA
 
@@ -489,6 +506,7 @@
         out_specs=[anywhere] * 2,
         scratch_shapes=[
             *[pltpu.VMEM(a.shape, a.dtype) for a in operands],
+            pltpu.VMEM((ROWS * LEVELS, COLS), F32),
             pltpu.VMEM((8, 8, SPAN), F32),
             pltpu.VMEM((8, SPAN, 1), F32),
             pltpu.VMEM((LEVELS * LEVEL, D), BF16),
@@ -503,10 +521,10 @@
             *pieces(), *pieces(), *pieces(), *pieces(),
             dma((len(operands),)), dma((5,)),
             dma((10,)), dma((11,)), dma((2, 4, 4)), dma((2, 4, 4)), dma((2, 4, 4)), dma((2, 4, 4)),
-            dma((3,)), dma((3,)), dma((3,)), dma((3,)),
+            dma((3, 2)), dma((3, 2)), dma((3, 2)), dma((3, 2)),
         ],
         compiler_params=pltpu.CompilerParams(
-            collective_id=0, has_side_effects=True, vmem_limit_bytes=56 * 1024 * 1024
+            collective_id=0, has_side_effects=True, vmem_limit_bytes=34 * 1024 * 1024
         ),
         name="attention_block",
     )(*operands)

time: 65.3 us -> 58 us (0.89)
  Pallas kernels: 58.3 us -> 55 us
  local copies, waits for them, and re-layouts: 2.71 us -> 0.01 us
  matrix products: 3.22 us -> 1.82 us
    pallas_call x1, Pallas kernels: 58.3 us -> 55 us  [local(): pl.pallas_call(kernel, out_shape=[jax.ShapeDtypeStruct(flat.shape, BF16),...]
    unnamed x4 -> x2, local copies, waits for them, and re-layouts: 2.71 us -> 0.01 us
    dot_general x1, matrix products: 3.22 us -> 1.82 us  [nt(): lax.dot_general(a, b, (((1,), (1,)), ((), ())), preferred_element_type=F32)]
where the time goes in v3:
time: 58 us; the launch traced here: 56.9 us
  Pallas kernels  55 us (95%)
  matrix products  1.82 us (3%)
    pallas_call x1, Pallas kernels, local(): pl.pallas_call(kernel, out_shape=[jax.ShapeDtypeStruct(flat.shape, BF16),...  55 us
    dot_general x1, matrix products, nt(): lax.dot_general(a, b, (((1,), (1,)), ((), ())), preferred_element_type=F32)  1.82 us

profile of v3, /device:TPU:6, one launch (start us, length us, event | category | flops | bytes accessed | tf_op | source)
XLA Modules:
  0.0 56.9 jit_solution(2252361733476451789)
XLA Ops:
  0.0 0.0 copy-start
  0.0 55.0 %attention_block.1 = (bf16[1152,512]{1,0:T(8,128)(2,1)S(1)}, bf16[512,512]{1,0:T(8,128)(2,1)S(1)}) custom-call(bf16[1152,512]{1,0:T(8,128)(2,1)} %bitcast.6, s32[12,4,24]{2,1,0:T(4,128)} %bitcast.8, bf16[32,48]{1,0:T(8,128)(2,1)} %qkv_in.1, bf16[16,32]{1,0:T(8,128)(2,1)} %bitcast.9, bf16[272,576]{1,0:T(8,128)(2,1)} %constant.18.clone.packs_in, ...), custom_call_target="tpu_custom_call" | custom-call | tf_op jit(solution)/shard_map/attention_block/pallas_call | solution.py:502
  55.0 0.0 copy-done
  55.0 1.8 %fusion = bf16[1152,512]{1,0:T(8,128)(2,1)} fusion(bf16[1152,512]{1,0:T(8,128)(2,1)S(1)} %get-tuple-element.7, bf16[512,512]{1,0:T(8,128)(2,1)S(1)} %get-tuple-element.8, bf16[1152,512]{1,0:T(8,128)(2,1)S(1)} %bitcast.7), kind=kOutput, calls=%fused_computation.1 | convolution fusion | flops 605749248 | bytes 4063232 | tf_op jit(solution)/shard_map/dot_general | solution.py:102
Async XLA Ops:
  0.0 55.0 %copy-start = (bf16[4,12,24,512]{3,2,1,0:T(8,128)(2,1)S(1)}, bf16[4,12,24,512]{3,2,1,0:T(8,128)(2,1)}, u32[]{:S(2)}) copy-start(bf16[4,12,24,512]{3,2,1,0:T(8,128)(2,1)} %param.13) | copy-start | bytes 3538948

commit v4 on v3

--- a/solution.py
+++ b/solution.py
@@ -125,24 +125,19 @@
     def along_z(step):
         return at(x, y, (z + step + 16) % 16, core)
 
-    def one_way(d):
-        return at((x + d) % 4, y, z, core)
-
-    def other_way(d):
-        return at(x, (y + d) % 4, z, core)
+    def one_way(part, d):
+        turn = part * core
+        return at((x + d * (1 - turn)) % 4, (y + d * turn) % 4, z, core)
+
+    def other_way(part, d):
+        turn = part * core
+        return at((x + d * turn) % 4, (y + d * (1 - turn)) % 4, z, core)
 
     def beside(d_lat, d_lon):
         return ((lat + d_lat + 16) % 16, (lon + d_lon + 32) % 32)
 
     peer = at(x, y, z, 1 - core)
-    near = [s for s in RELATIVE if 0 < abs(s) <= 4]
-    partners = [along_z(s) for s in near]
-    partners += [one_way(d) for d in (1, 2, 3)] + [other_way(d) for d in (1, 2, 3)] + [peer]
-    partners += [beside(a, b) for a, b in ((0, 1), (0, -1), (1, 0), (-1, 0), (1, 1), (-1, -1))]
-    barrier = pltpu.get_barrier_semaphore()
-    for partner in partners:
-        pl.semaphore_signal(barrier, 1, device_id=partner, device_id_type=MESH)
-
+    near = [4, -4, 3, -3, 2, -2, 1, -1]
     loads = [
         pltpu.make_async_copy(src, dst, in_sem.at[n])
         for n, (src, dst) in enumerate((
@@ -151,7 +146,17 @@
             (moves_in, moves), (sides_t_in, sides_t), (gathers_t_in, gathers_t), (packs_t_in, packs_t),
         ))
     ]
-    for load in loads:
+    for load in loads[:2]:
+        load.start()
+
+    partners = [along_z(s) for s in near]
+    partners += [one_way(0, d) for d in (1, 2, 3)] + [other_way(0, d) for d in (1, 2, 3)] + [peer]
+    partners += [beside(a, b) for a, b in ((0, 1), (0, -1), (1, 0), (-1, 0), (1, 1), (-1, -1))]
+    barrier = pltpu.get_barrier_semaphore()
+    for partner in partners:
+        pl.semaphore_signal(barrier, 1, device_id=partner, device_id_type=MESH)
+
+    for load in loads[2:]:
         load.start()
 
     loads[0].wait()
@@ -203,7 +208,7 @@
                 total += nn(chosen, slab(pair, part, start, height))
             buf[pl.ds(pair * size, size), :] = total.astype(BF16)
 
-    halos = []
+    halos = {}
 
     def send_halo(n, pair):
         src, dst, size, target = (
@@ -212,7 +217,7 @@
         rows = pl.ds(pair * size, size)
         copy = remote(src.at[rows, :], dst.at[rows, :], halo_send.at[n, pair], halo_recv.at[n, pair], target)
         copy.start()
-        halos.append(copy)
+        halos[n, pair] = copy
 
     send_halo(0, 0)
     send_halo(2, 0)
@@ -231,13 +236,13 @@
     def step_one(part, d):
         span = pl.ds(*PARTS[part])
         return remote(
-            raw.at[0, 0, 0, span], raw.at[0, 4 - d, 0, span], p_send.at[part, d, 0], p_recv.at[part, 4 - d, 0], one_way(d)
+            raw.at[0, 0, 0, span], raw.at[0, 4 - d, 0, span], p_send.at[part, d, 0], p_recv.at[part, 4 - d, 0], one_way(part, d)
         )
 
     def step_two(part, i, d):
         span = pl.ds(*PARTS[part])
         return remote(
-            raw.at[0, i, 0, span], raw.at[0, i, 4 - d, span], p_send.at[part, i, d], p_recv.at[part, i, 4 - d], other_way(d)
+            raw.at[0, i, 0, span], raw.at[0, i, 4 - d, span], p_send.at[part, i, d], p_recv.at[part, i, 4 - d], other_way(part, d)
         )
 
     def arrival(part, i, k):
@@ -253,16 +258,16 @@
         )
 
     def begin(part):
-        for d in (1, 3, 2):
+        for d in (2, 1, 3):
             step_one(part, d).start()
-        for d in (1, 3, 2):
+        for d in (2, 1, 3):
             step_two(part, 0, d).start()
         relay(part, 0, 0).start()
 
     def forward(part):
         for i in (1, 3, 2):
             arrival(part, i, 0).wait_recv()
-            for d in (1, 3, 2):
+            for d in (2, 1, 3):
                 step_two(part, i, d).start()
             relay(part, i, 0).start()
 
@@ -285,7 +290,8 @@
                 for member in range(4):
                     y_lo, cc = member // 2, member % 2
                     d_x, d_y = (x_hi * 2 + x_lo - x + 4) % 4, (y_hi * 2 + y_lo - y + 4) % 4
-                    piece = raw[(cc + core) % 2, d_x, d_y, pl.ds(start, count)].reshape(count * 16, 128)
+                    i, k = (d_y, d_x) if part * cc else (d_x, d_y)
+                    piece = raw[(cc + core) % 2, i, k, pl.ds(start, count)].reshape(count * 16, 128)
                     total += nn(piece, moves[member])
                 total = total.astype(BF16)
                 lanes = pl.ds(group * 128, 128)
@@ -327,12 +333,11 @@
     def _(i):
         pass_on(0, i)
 
-    loads[7].wait()
-    loads[8].wait()
-    for copy in halos:
-        copy.wait_recv()
     sizes = (112, 112, 48)
-    for pair in range(2):
+
+    def gather_windows(pair):
+        for n in range(3):
+            halos[n, pair].wait_recv()
         for w in range(4):
             start, height = SLABS[w]
             total = 0.0
@@ -346,6 +351,9 @@
                     )
             windows[pl.ds(place(w, pair) * SPAN, SPAN), :] = total.astype(BF16)
 
+    loads[7].wait()
+    loads[8].wait()
+    gather_windows(0)
     pass_on(1, 0)
     loads[9].wait()
     unpack(0)
@@ -354,6 +362,7 @@
     def _(i):
         pass_on(1, i)
 
+    gather_windows(1)
     unpack(1)
     proj_copy = pltpu.make_async_copy(whole_proj, proj_out, out_sem.at[4])
     proj_copy.start()
@@ -387,7 +396,7 @@
             bottom = jnp.where(lower, mixed[:SPAN, 128:], mixed[SPAN:, 128:])
             attended[w, :, pl.ds(t * 128, 128)] = (top / bottom).astype(BF16)
 
-    returns = []
+    returns = {}
 
     def give_back(k, sources, pair, target):
         total = 0.0
@@ -398,13 +407,13 @@
         src[rows, :] = total.astype(BF16)
         copy = remote(src.at[rows, :], dst.at[rows, :], back_send.at[k, pair], back_recv.at[k, pair], target)
         copy.start()
-        returns.append(copy)
+        returns[k, pair] = copy
 
     loads[10].wait()
     for pair in range(2):
         project_in(2 * pair, 2)
 
-        @pl.loop(2 * pair, 2 * pair + 2)
+        @pl.loop(2 * pair, 2 * pair + 2, unroll=2)
         def _(w):
             attend(w)
 
@@ -413,14 +422,14 @@
 
     project_in(4, 4)
 
-    @pl.loop(4, 6)
+    @pl.loop(4, 6, unroll=2)
     def _(w):
         attend(w)
 
     for pair in range(2):
         give_back(1, (0, 2), pair, beside(1, 0))
 
-    @pl.loop(6, 8)
+    @pl.loop(6, 8, unroll=2)
     def _(w):
         attend(w)
 
@@ -433,10 +442,10 @@
             restored[own_level(pair, part)] = total
 
     loads[12].wait()
-    for copy in returns:
-        copy.wait_recv()
     written = [proj_copy]
     for pair in range(2):
+        for k in (1, 2, 0):
+            returns[k, pair].wait_recv()
         for part in range(2):
             level = own_level(pair, part)
             total = restored[level]
@@ -451,7 +460,7 @@
             copy.start()
             written.append(copy)
 
-    for copy in first + far + halos + returns:
+    for copy in [*first, *far, *halos.values(), *returns.values()]:
         copy.wait_send()
     for part in range(2):
         for d in (1, 2, 3):

time: 58 us -> 56 us (0.966)
  Pallas kernels: 55 us -> 53.3 us
    pallas_call x1, Pallas kernels: 55 us -> 53.3 us  [local(): pl.pallas_call(kernel, out_shape=[jax.ShapeDtypeStruct(flat.shape, BF16),...]
where the time goes in v4:
time: 56 us; the launch traced here: 55.2 us
  Pallas kernels  53.3 us (95%)
  matrix products  1.82 us (3%)
    pallas_call x1, Pallas kernels, local(): pl.pallas_call(kernel, out_shape=[jax.ShapeDtypeStruct(flat.shape, BF16),...  53.3 us
    dot_general x1, matrix products, nt(): lax.dot_general(a, b, (((1,), (1,)), ((), ())), preferred_element_type=F32)  1.82 us

profile of v4, /device:TPU:6, one launch (start us, length us, event | category | flops | bytes accessed | tf_op | source)
XLA Modules:
  0.0 55.2 jit_solution(11426971772338977665)
XLA Ops:
  0.0 0.0 copy-start
  0.0 53.3 %attention_block.1 = (bf16[1152,512]{1,0:T(8,128)(2,1)S(1)}, bf16[512,512]{1,0:T(8,128)(2,1)S(1)}) custom-call(bf16[1152,512]{1,0:T(8,128)(2,1)} %bitcast.6, s32[12,4,24]{2,1,0:T(4,128)} %bitcast.8, bf16[32,48]{1,0:T(8,128)(2,1)} %qkv_in.1, bf16[16,32]{1,0:T(8,128)(2,1)} %bitcast.9, bf16[272,576]{1,0:T(8,128)(2,1)} %constant.18.clone.packs_in, ...), custom_call_target="tpu_custom_call" | custom-call | tf_op jit(solution)/shard_map/attention_block/pallas_call | solution.py:511
  53.3 0.0 copy-done
  53.3 1.8 %fusion = bf16[1152,512]{1,0:T(8,128)(2,1)} fusion(bf16[1152,512]{1,0:T(8,128)(2,1)S(1)} %get-tuple-element.7, bf16[512,512]{1,0:T(8,128)(2,1)S(1)} %get-tuple-element.8, bf16[1152,512]{1,0:T(8,128)(2,1)S(1)} %bitcast.7), kind=kOutput, calls=%fused_computation.1 | convolution fusion | flops 605749248 | bytes 4063232 | tf_op jit(solution)/shard_map/dot_general | solution.py:102
Async XLA Ops:
  0.0 53.3 %copy-start = (bf16[4,12,24,512]{3,2,1,0:T(8,128)(2,1)S(1)}, bf16[4,12,24,512]{3,2,1,0:T(8,128)(2,1)}, u32[]{:S(2)}) copy-start(bf16[4,12,24,512]{3,2,1,0:T(8,128)(2,1)} %param.13) | copy-start | bytes 3538948

commit v5 on v4

--- a/solution.py
+++ b/solution.py
@@ -83,7 +83,7 @@
 
 
 def place(w, pair):
-    return pair * 2 + w if w < 2 else w * 2 + pair
+    return pair * 3 + w if w < 3 else 6 + pair
 
 
 def own_level(pair, part):
@@ -146,7 +146,7 @@
             (moves_in, moves), (sides_t_in, sides_t), (gathers_t_in, gathers_t), (packs_t_in, packs_t),
         ))
     ]
-    for load in loads[:2]:
+    for load in loads[:4]:
         load.start()
 
     partners = [along_z(s) for s in near]
@@ -156,7 +156,7 @@
     for partner in partners:
         pl.semaphore_signal(barrier, 1, device_id=partner, device_id_type=MESH)
 
-    for load in loads[2:]:
+    for load in loads[4:]:
         load.start()
 
     loads[0].wait()
@@ -185,28 +185,8 @@
         first.append(copy)
     loads[2].wait()
 
-    @pl.loop(0, LEVELS)
-    def _(i):
-        rows = pl.ds(pl.multiple_of(i * LEVEL, LEVEL), LEVEL)
-        floated = tokens[rows, :].astype(F32)
-        average = jnp.mean(floated, axis=-1, keepdims=True)
-        centred = floated - average
-        spread = jnp.mean(centred * centred, axis=-1, keepdims=True)
-        normed[rows, :] = (centred * lax.rsqrt(spread + EPS)).astype(BF16)
-
     def slab(pair, part, start, size):
         return normed[pl.ds(own_level(pair, part) * LEVEL + start, size), :]
-
-    loads[3].wait()
-    for pair in range(2):
-        for buf, begins, size, start, height in (
-            (w_out, 0, 112, 64, 224), (n_out, 112, 112, 0, 80), (c_out, 224, 48, 0, 80),
-        ):
-            total = 0.0
-            for part in range(2):
-                chosen = packs[pl.ds(begins, size), pl.ds(part * LEVEL, LEVEL)][:, start:start + height]
-                total += nn(chosen, slab(pair, part, start, height))
-            buf[pl.ds(pair * size, size), :] = total.astype(BF16)
 
     halos = {}
 
@@ -219,10 +199,31 @@
         copy.start()
         halos[n, pair] = copy
 
-    send_halo(0, 0)
-    send_halo(2, 0)
-    send_halo(1, 0)
-    send_halo(1, 1)
+    loads[3].wait()
+    for pair in range(2):
+
+        @pl.loop(0, 2)
+        def _(part):
+            rows = pl.ds(pl.multiple_of(own_level(pair, part) * LEVEL, LEVEL), LEVEL)
+            floated = tokens[rows, :].astype(F32)
+            average = jnp.mean(floated, axis=-1, keepdims=True)
+            centred = floated - average
+            spread = jnp.mean(centred * centred, axis=-1, keepdims=True)
+            normed[rows, :] = (centred * lax.rsqrt(spread + EPS)).astype(BF16)
+
+        for buf, begins, size, start, height in (
+            (w_out, 0, 112, 64, 224), (c_out, 224, 48, 0, 80), (n_out, 112, 112, 0, 80),
+        ):
+            total = 0.0
+            for part in range(2):
+                chosen = packs[pl.ds(begins, size), pl.ds(part * LEVEL, LEVEL)][:, start:start + height]
+                total += nn(chosen, slab(pair, part, start, height))
+            buf[pl.ds(pair * size, size), :] = total.astype(BF16)
+        if pair == 0:
+            send_halo(0, 0)
+            send_halo(2, 0)
+        send_halo(1, pair)
+
     for copy in first:
         copy.wait_recv()
 
@@ -362,7 +363,6 @@
     def _(i):
         pass_on(1, i)
 
-    gather_windows(1)
     unpack(1)
     proj_copy = pltpu.make_async_copy(whole_proj, proj_out, out_sem.at[4])
     proj_copy.start()
@@ -376,7 +376,7 @@
     ones = jnp.ones((SPAN, 128), BF16)
 
     def attend(w):
-        rows = pl.ds(pl.multiple_of(w * SPAN, 16), SPAN)
+        rows = pl.ds(w * SPAN if isinstance(w, int) else pl.multiple_of(w * SPAN, 16), SPAN)
         bias = jnp.where(tag_cols[w] == tag_rows[w][0:1], 0.0, -1e30)
         bias = jnp.concatenate([bias, bias], axis=0)
         scores = []
@@ -410,24 +410,27 @@
         returns[k, pair] = copy
 
     loads[10].wait()
-    for pair in range(2):
-        project_in(2 * pair, 2)
-
-        @pl.loop(2 * pair, 2 * pair + 2, unroll=2)
-        def _(w):
-            attend(w)
-
-        give_back(0, (0, 1), pair, beside(0, 1))
-        give_back(2, (0,), pair, beside(1, 1))
-
-    project_in(4, 4)
-
-    @pl.loop(4, 6, unroll=2)
+    project_in(0, 2)
+
+    @pl.loop(0, 2, unroll=2)
     def _(w):
         attend(w)
 
-    for pair in range(2):
-        give_back(1, (0, 2), pair, beside(1, 0))
+    give_back(0, (0, 1), 0, beside(0, 1))
+    give_back(2, (0,), 0, beside(1, 1))
+    gather_windows(1)
+    project_in(2, 4)
+
+    @pl.loop(2, 5, unroll=3)
+    def _(w):
+        attend(w)
+
+    give_back(0, (0, 1), 1, beside(0, 1))
+    give_back(2, (0,), 1, beside(1, 1))
+    give_back(1, (0, 2), 0, beside(1, 0))
+    attend(5)
+    give_back(1, (0, 2), 1, beside(1, 0))
+    project_in(6, 2)
 
     @pl.loop(6, 8, unroll=2)
     def _(w):

time: 56 us -> 55.5 us (level)
  the two profiles are of different devices: /device:TPU:6 before, /device:TPU:1 now
where the time goes in v5:
time: 55.5 us; the launch traced here: 55.4 us
  Pallas kernels  53.5 us (96%)
  matrix products  1.82 us (3%)
    pallas_call x1, Pallas kernels, local(): pl.pallas_call(kernel, out_shape=[jax.ShapeDtypeStruct(flat.shape, BF16),...  53.5 us
    dot_general x1, matrix products, nt(): lax.dot_general(a, b, (((1,), (1,)), ((), ())), preferred_element_type=F32)  1.82 us

profile of v5, /device:TPU:1, one launch (start us, length us, event | category | flops | bytes accessed | tf_op | source)
XLA Modules:
  0.0 55.4 jit_solution(11506955230235668447)
XLA Ops:
  0.0 0.0 copy-start
  0.0 53.5 %attention_block.1 = (bf16[1152,512]{1,0:T(8,128)(2,1)S(1)}, bf16[512,512]{1,0:T(8,128)(2,1)S(1)}) custom-call(bf16[1152,512]{1,0:T(8,128)(2,1)} %bitcast.6, s32[12,4,24]{2,1,0:T(4,128)} %bitcast.8, bf16[32,48]{1,0:T(8,128)(2,1)} %qkv_in.1, bf16[16,32]{1,0:T(8,128)(2,1)} %bitcast.9, bf16[272,576]{1,0:T(8,128)(2,1)} %constant.18.clone.packs_in, ...), custom_call_target="tpu_custom_call" | custom-call | tf_op jit(solution)/shard_map/attention_block/pallas_call | solution.py:514
  53.5 0.0 copy-done
  53.6 1.8 %fusion = bf16[1152,512]{1,0:T(8,128)(2,1)} fusion(bf16[1152,512]{1,0:T(8,128)(2,1)S(1)} %get-tuple-element.7, bf16[512,512]{1,0:T(8,128)(2,1)S(1)} %get-tuple-element.8, bf16[1152,512]{1,0:T(8,128)(2,1)S(1)} %bitcast.7), kind=kOutput, calls=%fused_computation.1 | convolution fusion | flops 605749248 | bytes 4063232 | tf_op jit(solution)/shard_map/dot_general | solution.py:102
Async XLA Ops:
  0.0 53.5 %copy-start = (bf16[4,12,24,512]{3,2,1,0:T(8,128)(2,1)S(1)}, bf16[4,12,24,512]{3,2,1,0:T(8,128)(2,1)}, u32[]{:S(2)}) copy-start(bf16[4,12,24,512]{3,2,1,0:T(8,128)(2,1)} %param.13) | copy-start | bytes 3538948
